TPU v7x, 512 devices: a whole 4x4x16 slice. The times are simulated.
512 devices in a mesh: ctx: 32 (over y, z_lo), head: 16 (over z_hi, x, core).
Axes of the slice: x: 4, y: 4, z: 16 (z_hi: 2, z_lo: 8; z = z_hi * 8 + z_lo), core: 2. Of those that a mesh axis runs over, the one named last changes fastest.
Arguments:
- query_rows: bfloat16 [12288, 16, 128], P('ctx', 'head'), may hold values from -5 to 5
- key_rows: bfloat16 [12288, 16, 128], P('ctx', 'head'), may hold values from -5 to 5
- value_rows: bfloat16 [12288, 16, 128], P('ctx', 'head'), may hold values from -6 to 6
- out_weight: bfloat16 [2048, 2048], P('head'), may hold values from -0.1875 to 0.1875
Outputs:
- projected: bfloat16 [12288, 2048], P('ctx', 'head')
All inputs are finite; a program needn't handle non-finite values.
Results may differ from a plain program's by a relative error of at most 0.0058.
Values may be sent and summed in bfloat16 or wider, within the bound.
No kernel may reach another device: no remote copies, remote signals or barrier semaphores. Data moves between devices by JAX's collectives and lax.ppermute only.
A program may use at most 64 MiB of HBM per device.

v0:
```python
import jax
import jax.numpy as jnp
from jax import lax
from jax.sharding import PartitionSpec as P


def score_block(query_part, key_part):
    return jnp.einsum(
        "qhd,khd->hqk", query_part, key_part, preferred_element_type=jnp.float32
    ) * query_part.shape[-1] ** (-0.5)


def blockwise(step, running, pieces):
    row_count = pieces[0].shape[0]
    block_len = 1024
    stacked = tuple((p.reshape((row_count // block_len, block_len) + p.shape[1:]) for p in pieces))

    def advance(state, item):
        blocks, number = item
        return (step(state, blocks, number * block_len), None)

    result, unused = lax.scan(
        advance, running, (stacked, jnp.arange(row_count // block_len, dtype=jnp.int32))
    )
    return result


def shards(query_rows, key_rows, value_rows, out_weight):
    tok_local = query_rows.shape[0]
    head_local = query_rows.shape[1]

    def row_step(state, blocks, offset):
        row_peak, row_total = state
        scores = score_block(query_rows, blocks[0])
        new_peak = jnp.maximum(row_peak, jnp.max(scores, axis=2))
        row_total = row_total * jnp.exp(row_peak - new_peak) + jnp.sum(
            jnp.exp(scores - new_peak[:, :, None]), axis=2
        )
        return (new_peak, row_total)

    start_stats = (
        jnp.full((head_local, tok_local), -jnp.inf, jnp.float32),
        jnp.zeros((head_local, tok_local), jnp.float32),
    )
    row_peak, row_total = blockwise(
        row_step, start_stats, (lax.all_gather(key_rows, "ctx", axis=0, tiled=True),)
    )

    def weighted(attended_sum, key_part, value_part, scale_part):
        scores = score_block(query_rows, key_part)
        shares = jnp.exp(scores - row_peak[:, :, None]) / row_total[:, :, None]
        weights = (shares / scale_part.T[:, None, :]).astype(jnp.bfloat16)
        return attended_sum + jnp.einsum(
            "hqk,khd->hqd", weights, value_part, preferred_element_type=jnp.float32
        )

    start_sum = jnp.zeros((head_local, tok_local, query_rows.shape[2]), jnp.float32)
    whole_columns = tok_local * lax.axis_size("ctx")

    def placed(inner, blocks, offset):
        scores = score_block(query_rows, blocks[0])
        shares = jnp.exp(scores - row_peak[:, :, None]) / row_total[:, :, None]
        return lax.dynamic_update_slice_in_dim(inner, jnp.sum(shares, axis=1), offset, 1)

    partials = blockwise(
        placed,
        jnp.zeros((head_local, whole_columns), jnp.float32),
        (lax.all_gather(key_rows, "ctx", axis=0, tiled=True),),
    )
    column_sum = lax.psum_scatter(partials, "ctx", scatter_dimension=1, tiled=True)

    def apply_block(inner, blocks, offset):
        return weighted(inner, blocks[0], blocks[1], blocks[2])

    attended_sum = blockwise(
        apply_block,
        start_sum,
        (
            lax.all_gather(key_rows.astype(jnp.float32), "ctx", axis=0, tiled=True).astype(
                jnp.bfloat16
            ),
            lax.all_gather(value_rows.astype(jnp.float32), "ctx", axis=0, tiled=True).astype(
                jnp.bfloat16
            ),
            lax.all_gather(column_sum.T, "ctx", axis=0, tiled=True),
        ),
    )
    attended = attended_sum.astype(jnp.bfloat16)
    flat = jnp.transpose(attended, (1, 0, 2)).reshape(tok_local, head_local * query_rows.shape[2])
    partial_out = jnp.dot(flat, out_weight, preferred_element_type=jnp.float32)
    return lax.psum_scatter(partial_out, "head", scatter_dimension=1, tiled=True).astype(
        jnp.bfloat16
    )


def solution(mesh):
    placed = (
        P("ctx", "head", None),
        P("ctx", "head", None),
        P("ctx", "head", None),
        P("head", None),
    )
    return jax.shard_map(
        shards, mesh=mesh, in_specs=placed, out_specs=P("ctx", "head"), check_vma=False
    )
```

profile of v0, /device:TPU:8, one launch (start us, length us, event | category | flops | bytes accessed | tf_op | source)
XLA Modules:
  0.0 1196.2 jit_solution(13491327695195767850)
XLA Ops:
  7.3 221.4 %all-gather.7.cloned.1.call-done = bf16[12288,1,128]{2,0,1:T(8,128)(2,1)} async-done(((bf16[384,1,128]{2,0,1:T(8,128)(2,1)}), bf16[12288,1,128]{2,0,1:T(8,128)(2,1)}) %all-gather.7.cloned.1.call-update) | async-done | bytes 3145744 | tf_op jit(solution)/shard_map/all_gather | solution.py:68
  228.7 20.6 %while.35 = (s32[]{:T(128)}, f32[1,384]{1,0:T(1,128)S(1)}, f32[1,384]{1,0:T(1,128)S(1)}, bf16[12,1024,1,128]{3,1,2,0:T(8,128)(2,1)}, bf16[384,1,128]{2,0,1:T(8,128)(2,1)}, /*index=5*/s32[]{:T(128)}, s32[]{:T(128)}) while((s32[]{:T(128)}, f32[1,384]{1,0:T(1,128)S(1)}, f32[1,384]{1,0:T(1,128)S(1)}, ...), condition=%wide.region_3.4_spmd.clone, body=%wide.region_0.3_spmd.clone.sunk | while | flops 102238080 | bytes 3528280 | solution.py:22
  228.7 1.3 fusion.49
  230.4 1.4 fusion.49
  232.1 1.4 fusion.49
  233.8 1.4 fusion.49
  235.6 1.4 fusion.49
  237.3 1.4 fusion.49
  239.0 1.4 fusion.49
  240.7 1.4 fusion.49
  242.4 1.4 fusion.49
  244.2 1.4 fusion.49
  245.9 1.4 fusion.49
  247.6 1.4 fusion.49
  249.4 32.0 %while.34 = (s32[]{:T(128)}, f32[1,12288]{1,0:T(1,128)S(1)}, bf16[12,1024,1,128]{3,1,2,0:T(8,128)(2,1)}, bf16[384,1,128]{2,0,1:T(8,128)(2,1)}, f32[1,384]{1,0:T(...) while((s32[]{:T(128)}, f32[1,12288]{1,0:T(1,128)S(1)}, ...), condition=%wide.region_6.7_spmd, body=%wide.region_4.6_spmd.sunk | while | flops 102235136 | bytes 382651 | solution.py:22
  250.5 1.5 fusion.48
  253.2 1.5 fusion.48
  255.9 1.5 fusion.48
  258.5 1.5 fusion.48
  261.2 1.5 fusion.48
  263.9 1.5 fusion.48
  266.5 1.5 fusion.48
  269.2 1.5 fusion.48
  271.9 1.5 fusion.48
  274.5 1.5 fusion.48
  277.2 1.5 fusion.48
  279.9 1.5 fusion.48
  281.4 4.0 copy.19
  286.8 257.4 %reduce-scatter.7.cloned.1.call-done = f32[384,1]{1,0:T(8,128)} async-done(((f32[12288,1]{1,0:T(8,128)}), f32[384,1]{1,0:T(8,128)}) %reduce-scatter.7.cloned.1.call-update) | async-done | bytes 1552
  545.2 105.4 %all-gather = f32[1,12288]{1,0:T(1,128)S(1)} all-gather(f32[1,384]{1,0:T(1,128)S(1)} %copy.20), channel_id=2, replica_groups=mesh['ctx'=32,'head'=16] {'ctx'}, dimensions={1}, use_global_device_ids=true | all-gather | bytes 50688 | tf_op jit(solution)/shard_map/all_gather | solution.py:85
  650.6 122.8 %all-gather.9.cloned.1.call-done = bf16[12288,1,128]{2,0,1:T(8,128)(2,1)} async-done(((bf16[384,1,128]{2,0,1:T(8,128)(2,1)}), bf16[12288,1,128]{2,0,1:T(8,128)(2,1)}) %all-gather.9.cloned.1.call-update) | async-done | bytes 3145744 | tf_op jit(solution)/shard_map/all_gather | solution.py:82
  773.4 233.1 %all-gather.5.cloned.1.call-done = bf16[12288,1,128]{2,0,1:T(8,128)(2,1)} async-done(((bf16[384,1,128]{2,0,1:T(8,128)(2,1)}), bf16[12288,1,128]{2,0,1:T(8,128)(2,1)}) %all-gather.5.cloned.1.call-update) | async-done | bytes 3145744 | tf_op jit(solution)/shard_map/all_gather | solution.py:79
  1006.5 25.2 %while.36 = (s32[]{:T(128)}, f32[1,384,128]{2,1,0:T(8,128)S(1)}, bf16[12,1024,1,128]{3,1,2,0:T(8,128)(2,1)}, bf16[384,1,128]{2,0,1:T(8,128)(2,1)S(1)}, f32[1,384...) while((s32[]{:T(128)}, f32[1,384,128]{2,1,0:T(8,128)S(1)}, ...), condition=%wide.region_9.10_spmd.clone, body=%wide.region_8.9_spmd.clone.sunk | while | flops 203390976 | bytes 1038467 | solution.py:22
  1006.6 2.0 fusion.55
  1008.7 2.0 fusion.55
  1010.8 2.0 fusion.55
  1012.9 2.0 fusion.55
  1015.0 2.0 fusion.55
  1017.1 2.0 fusion.55
  1019.2 2.0 fusion.55
  1021.3 2.0 fusion.55
  1023.4 2.0 fusion.55
  1025.5 2.0 fusion.55
  1027.6 2.0 fusion.55
  1029.7 2.0 fusion.55
  1031.7 2.2 fusion.30
  1034.0 154.2 %reduce-scatter.5.cloned.1.call-done = f32[384,128]{1,0:T(8,128)} async-done(((f32[384,2048]{1,0:T(8,128)}), f32[384,128]{1,0:T(8,128)}) %reduce-scatter.5.cloned.1.call-update) | async-done | bytes 196624 | tf_op jit(solution)/shard_map/reduce_scatter | solution.py:91
  1188.1 1.6 convert_element_type.27
  (152 shorter events, 15.0 us)
Async XLA Ops:
  6.5 1025.2 %copy-start = (bf16[128,2048]{1,0:T(8,128)(2,1)S(1)}, bf16[128,2048]{1,0:T(8,128)(2,1)}, u32[]{:S(2)}) copy-start(bf16[128,2048]{1,0:T(8,128)(2,1)} %param.13) | copy-start | bytes 1572868
  6.5 222.1 %all-gather.7.cloned.1.call-start = ((), (), s32[]{:S(2)}) async-start(), calls=%async_computation.3 | async-start | bytes 3244032 | tf_op jit(solution)/shard_map/all_gather | solution.py:68
  7.3 536.9 %reduce-scatter.7.cloned.1.call-start = ((), (), s32[]{:S(2)}) async-start(), calls=%async_computation.6 | async-start | bytes 6488064
  285.4 721.1 %copy-start.1 = (bf16[384,1,128]{2,0,1:T(8,128)(2,1)S(1)}, bf16[384,1,128]{2,0,1:T(8,128)(2,1)}, u32[]{:S(2)}) copy-start(bf16[384,1,128]{2,0,1:T(8,128)(2,1)} %get-tuple-element.496) | copy-start | bytes 294916
  285.4 488.0 %all-gather.9.cloned.1.call-start = ((), (), s32[]{:S(2)}) async-start(), calls=%async_computation.4 | async-start | bytes 3244032 | tf_op jit(solution)/shard_map/all_gather | solution.py:82
  286.2 720.4 %all-gather.5.cloned.1.call-start = ((), (), s32[]{:S(2)}) async-start(), calls=%async_computation.2 | async-start | bytes 3244032 | tf_op jit(solution)/shard_map/all_gather | solution.py:79
  286.7 901.4 %reduce-scatter.5.cloned.1.call-start = ((), (), s32[]{:S(2)}) async-start(), calls=%async_computation.5 | async-start | bytes 3342336 | tf_op jit(solution)/shard_map/reduce_scatter | solution.py:91
Sparse Core Ops, SparseCore 0:
  9.4 219.1 all-gather.6
  285.5 258.6 reduce-scatter.6
  546.3 227.0 all-gather.8
  775.4 231.1 all-gather.4
  1034.1 154.0 reduce-scatter.4
where the time goes:
time: 1200 us
  waiting for transfers between devices  991 us (83%)
  blocking collectives  105 us (9%)
  matrix products  60.4 us (5%)
  between operations  13.2 us (1%)
    unnamed x6, waiting for transfers between devices  259 us
    all_gather x1, waiting for transfers between devices, shards(): lax.all_gather(key_rows.astype(jnp.float32), 'ctx', axis=0, tiled=True)  233 us
    all_gather x1, waiting for transfers between devices, shards(): lax.all_gather(key_rows, 'ctx', axis=0, tiled=True)  221 us
    reduce_scatter x1, waiting for transfers between devices, shards(): lax.psum_scatter(partial_out, 'head', scatter_dimension=1, tiled=True)  154 us
    all_gather x1, waiting for transfers between devices, shards(): lax.all_gather(value_rows.astype(jnp.float32), 'ctx', axis=0, tiled=True)  123 us
    all_gather x1, blocking collectives, shards(): lax.all_gather(column_sum.T, 'ctx', axis=0, tiled=True)  105 us
    dot_general x24, matrix products, score_block(): jnp.einsum('qhd,khd->hqk', query_part, key_part, preferred_element_type=j...  34 us
    dot_general x12, matrix products, weighted(): jnp.einsum('hqk,khd->hqd', weights, value_part, preferred_element_type=jn...  24.2 us
  transfers between devices with their start and end apart: 5, of which 5 were waited for; matrix products, arithmetic and copies ran while one was open for 0% of the time, Pallas kernels for 0%

commit v1 on v0

v1 whole, which is shorter than its diff:
```python
import functools
import math

import jax
import jax.numpy as jnp
from jax import lax
from jax.experimental import pallas as pl
from jax.experimental.pallas import tpu as pltpu
from jax.sharding import PartitionSpec as P

F32 = jnp.float32
BF16 = jnp.bfloat16
ROWS = 384
DIM = 128
QB = 4
KB = 8
HALF = 4 * ROWS
KEY_BITS = ((0, 2, 4, 6), (1, 3, 5, 7))
QUERY_BITS = (0, 2, 1, 3)
GROUPS = ROWS // 128
SUB = 128
EXP_SCALE = DIM ** -0.5 * math.log2(math.e)
LIFT = 2.0 ** 20
NT = (((1,), (1,)), ((), ()))
VMEM = pl.BlockSpec(memory_space=pltpu.VMEM)


def ctx_send(value, dy=0, dza=0, dzb=0):
    step = dy * 8 + dza * 4 + dzb
    return lax.ppermute(value, "ctx", [(i, i ^ step) for i in range(32)])


def head_send(value, dzh=0, dx=0, dcore=0):
    step = dzh * 8 + dx * 2 + dcore
    return lax.ppermute(value, "head", [(i, i ^ step) for i in range(16)])


LINE = [[y * 8 + za * 4 + zb for zb in range(4)] for y in range(4) for za in range(2)]
PLANE = [[y * 8 + za * 4 + zb for y in range(4) for za in range(2)] for zb in range(4)]
ROW = [[zh * 8 + x * 2 + core for x in range(4)] for zh in range(2) for core in range(2)]


def swap(value, axis, groups):
    return lax.all_to_all(value, axis, 0, 0, axis_index_groups=groups, tiled=True)


def columns_to_rows(columns):
    lane = lax.broadcasted_iota(jnp.int32, (128, 128), 1)
    square = jnp.zeros((128, 128), F32)
    for at, column in enumerate(columns):
        square = jnp.where(lane == at, column, square)
    return square.T[:8]


def rows_to_columns(rows):
    return jnp.concatenate([rows] * 16, axis=0).T


def gather_queries(u, q_refs, q_all):
    @pl.when(u == 0)
    def _():
        q_all[0] = q_refs[0][0]
        q_all[1] = q_refs[1][0]
        q_all[2] = q_refs[2][0]
        q_all[3] = q_refs[2][1]


def half_scores(u, q_all, kv_refs, e_ref, s_ref):
    peaks, totals = [], []
    for sub in range(GROUPS):
        q = q_all[u, sub * SUB : (sub + 1) * SUB, :]
        top = jnp.full((SUB, 128), -jnp.inf, F32)
        for b in range(4):
            s = lax.dot_general(q, kv_refs[b][0], NT, preferred_element_type=F32)
            s_ref[sub, :, b * ROWS : (b + 1) * ROWS] = s
            for g in range(GROUPS):
                top = jnp.maximum(top, s[:, g * 128 : (g + 1) * 128])
        peak = jnp.max(top, axis=1, keepdims=True)
        total = jnp.zeros((SUB, 128), F32)
        for b in range(4 * GROUPS):
            e = jnp.exp2((s_ref[sub, :, b * 128 : (b + 1) * 128] - peak) * EXP_SCALE)
            total = total + e
            e_ref[sub * SUB : (sub + 1) * SUB, b * 128 : (b + 1) * 128] = e.astype(BF16)
        peaks.append(peak)
        totals.append(jnp.sum(total, axis=1, keepdims=True))
    return columns_to_rows(peaks + totals)


def first_score_kernel(*refs):
    q_refs, kv_refs, (e_ref, stat_ref, q_all, s_ref) = refs[:3], refs[3:7], refs[7:]
    u = pl.program_id(0)
    gather_queries(u, q_refs, q_all)
    stat_ref[u] = half_scores(u, q_all, kv_refs, e_ref, s_ref)


def combine(a, b):
    peak = jnp.maximum(a[:GROUPS], b[:GROUPS])
    total = a[GROUPS : 2 * GROUPS] * jnp.exp2((a[:GROUPS] - peak) * EXP_SCALE)
    total = total + b[GROUPS : 2 * GROUPS] * jnp.exp2((b[:GROUPS] - peak) * EXP_SCALE)
    return jnp.concatenate([peak, total, jnp.zeros((8 - 2 * GROUPS, 128), F32)], axis=0)


def second_score_kernel(place_ref, *refs):
    q_refs, kv_refs, first_ref = refs[:3], refs[3:7], refs[7]
    e_ref, stat_ref, both_ref, q_all, s_ref = refs[8:]
    u = pl.program_id(0)
    gather_queries(u, q_refs, q_all)
    rows = half_scores(u, q_all, kv_refs, e_ref, s_ref)
    stat_ref[u] = rows
    rows = combine(first_ref[u], rows)
    at = place_ref[0] ^ ((u % 2) * 2 + u // 2)
    for to in range(QB):
        both_ref[to, at] = rows


SMEM = pl.BlockSpec(memory_space=pltpu.SMEM)
EXPO = pl.BlockSpec((ROWS, HALF), lambda u: (u, 0))
SCORE = dict(
    grid=(QB,),
    scratch_shapes=[pltpu.VMEM((QB, ROWS, DIM), BF16), pltpu.VMEM((GROUPS, SUB, HALF), F32)],
    compiler_params=pltpu.CompilerParams(vmem_limit_bytes=16 * 1024 * 1024),
)
EXPO_TYPE = jax.ShapeDtypeStruct((QB * ROWS, HALF), BF16)
STAT_TYPE = jax.ShapeDtypeStruct((QB, 8, 128), F32)


def first_scores(queries, pieces):
    return pl.pallas_call(
        first_score_kernel,
        in_specs=[VMEM] * 7,
        out_specs=[EXPO, VMEM],
        out_shape=[EXPO_TYPE, STAT_TYPE],
        **SCORE,
    )(*queries, *pieces)


def second_scores(place, queries, pieces, stats):
    return pl.pallas_call(
        second_score_kernel,
        in_specs=[SMEM] + [VMEM] * 8,
        out_specs=[EXPO, VMEM, VMEM],
        out_shape=[EXPO_TYPE, STAT_TYPE, jax.ShapeDtypeStruct((QB, QB, 8, 128), F32)],
        **SCORE,
    )(place, *queries, *pieces, stats)


def column_kernel(
    place_ref, e0_ref, e1_ref, stat0_ref, stat1_ref, all_ref, factor_ref, column_ref, sum_ref
):
    u = pl.program_id(0)

    @pl.when(u == 0)
    def _():
        for block in range(QB):
            at = place_ref[0] ^ QUERY_BITS[block]
            whole = functools.reduce(combine, [all_ref[j, at] for j in range(QB)])
            for half, stat_ref in enumerate((stat0_ref, stat1_ref)):
                mine = stat_ref[block]
                factor = jnp.exp2((mine[:GROUPS] - whole[:GROUPS]) * EXP_SCALE)
                factor = factor / whole[GROUPS : 2 * GROUPS]
                factor_ref[half, block] = jnp.concatenate(
                    [factor, jnp.zeros((8 - GROUPS, 128), F32)], axis=0
                )
        sum_ref[...] = jnp.zeros_like(sum_ref)

    at = lax.broadcasted_iota(jnp.int32, (16, ROWS), 0)
    for half, e_ref in enumerate((e0_ref, e1_ref)):
        mine = factor_ref[half, u]
        row = jnp.concatenate([mine[g : g + 1] for g in range(GROUPS)], axis=1)
        high = row.astype(BF16).astype(F32)
        left = jnp.where(at == 0, high, jnp.where(at == 1, row - high, 0.0)).astype(BF16)
        sum_ref[half] += jnp.dot(left, e_ref[...], preferred_element_type=F32)

    @pl.when(u == QB - 1)
    def _():
        for half in range(2):
            whole = sum_ref[half, 0:1] + sum_ref[half, 1:2]
            for b in range(4):
                row = whole[:, b * ROWS : (b + 1) * ROWS]
                column_ref[0, pl.ds(place_ref[1] ^ KEY_BITS[half][b], 1)] = row
        for to in range(1, KB):
            column_ref[to] = column_ref[0]


def columns(place, expos, stats, all_stats):
    return pl.pallas_call(
        column_kernel,
        grid=(QB,),
        in_specs=[SMEM, EXPO, EXPO, VMEM, VMEM, VMEM],
        out_specs=[VMEM, VMEM],
        out_shape=[
            jax.ShapeDtypeStruct((2, QB, 8, 128), F32),
            jax.ShapeDtypeStruct((KB, KB, ROWS), F32),
        ],
        scratch_shapes=[pltpu.VMEM((2, 16, HALF), F32)],
        compiler_params=pltpu.CompilerParams(vmem_limit_bytes=16 * 1024 * 1024),
    )(place, *expos, *stats, all_stats)


def value_kernel(place_ref, e0_ref, e1_ref, factor_ref, *refs):
    kv_refs, (sums_ref, out_ref, scaled, inverse) = refs[:KB], refs[KB:]
    u = pl.program_id(0)

    @pl.when(u == 0)
    def _():
        inverse[...] = (1.0 / LIFT) / functools.reduce(
            jnp.add, [sums_ref[j] for j in range(KB)]
        )
        bits = KEY_BITS[0] + KEY_BITS[1]
        rows = jnp.concatenate(
            [inverse[pl.ds(place_ref[1] ^ bit, 1)] for bit in bits], axis=0
        )
        for g in range(GROUPS):
            column = rows_to_columns(rows[:, g * 128 : (g + 1) * 128])
            for b in range(KB):
                part = kv_refs[b][1, g * 128 : (g + 1) * 128, :].astype(F32)
                scaled[b * ROWS + g * 128 : b * ROWS + (g + 1) * 128, :] = (
                    part * column[:, b : b + 1]
                ).astype(BF16)

    parts = []
    for half, e_ref in enumerate((e0_ref, e1_ref)):
        part = jnp.dot(
            e_ref[...], scaled[half * HALF : (half + 1) * HALF], preferred_element_type=F32
        )
        parts.append((part, rows_to_columns(factor_ref[half, u]) * LIFT))
    at = place_ref[0] ^ ((u % 2) * 2 + u // 2)
    for g in range(GROUPS):
        rows = slice(g * 128, (g + 1) * 128)
        out_ref[at, rows, :] = sum(
            part[rows] * column[:, g : g + 1] for part, column in parts
        ).astype(BF16)


def attend(place, expos, factor, pieces, sums):
    return pl.pallas_call(
        value_kernel,
        grid=(QB,),
        in_specs=[SMEM, EXPO, EXPO] + [VMEM] * (KB + 2),
        out_specs=VMEM,
        out_shape=jax.ShapeDtypeStruct((QB, ROWS, DIM), BF16),
        scratch_shapes=[pltpu.VMEM((2 * HALF, DIM), BF16), pltpu.VMEM((KB, ROWS), F32)],
        compiler_params=pltpu.CompilerParams(vmem_limit_bytes=16 * 1024 * 1024),
    )(place, *expos, factor, *pieces, sums)


def weight_kernel(place_ref, w_ref, *outs):
    zh, x, core = place_ref[2], place_ref[3], place_ref[4]
    for dx in range(4):
        for dcore in range(2):
            for dzh in range(2):
                to = (zh ^ dzh) * 8 + (x ^ dx) * 2 + (core ^ dcore)
                at = dcore * 2 + dzh
                outs[dx][:, at * 128 : (at + 1) * 128] = w_ref[
                    :, pl.ds(pl.multiple_of(to * 128, 128), 128)
                ]


def weight_parts(place, out_weight):
    return pl.pallas_call(
        weight_kernel,
        in_specs=[SMEM, VMEM],
        out_specs=[VMEM] * 4,
        out_shape=[jax.ShapeDtypeStruct((DIM, 512), BF16)] * 4,
        compiler_params=pltpu.CompilerParams(vmem_limit_bytes=8 * 1024 * 1024),
    )(place, out_weight)


def project_kernel(place_ref, rows_ref, *refs):
    weights, (keep_ref, send_ref) = refs[:4], refs[4:]
    total = jnp.zeros((ROWS, 512), F32)
    for bit in range(4):
        total = total + jnp.dot(
            rows_ref[place_ref[3] ^ bit], weights[bit][...], preferred_element_type=F32
        )
    keep_ref[...] = total[:, :256]
    send_ref[...] = total[:, 256:]


def project(place, rows, weights):
    return pl.pallas_call(
        project_kernel,
        in_specs=[SMEM] + [VMEM] * 5,
        out_specs=[VMEM] * 2,
        out_shape=[jax.ShapeDtypeStruct((ROWS, 256), F32)] * 2,
        compiler_params=pltpu.CompilerParams(vmem_limit_bytes=16 * 1024 * 1024),
    )(place, rows, *weights)


def shards(query_rows, key_rows, value_rows, out_weight):
    q, k, v = (rows.reshape(1, ROWS, DIM) for rows in (query_rows, key_rows, value_rows))
    ctx, head = lax.axis_index("ctx"), lax.axis_index("head")
    place = jnp.stack(
        [ctx % 4, ctx // 4, head // 8, head // 2 % 4, head % 2]
    ).astype(jnp.int32)
    pair, q, out_weight = lax.optimization_barrier((jnp.concatenate([k, v]), q, out_weight))
    far = ctx_send(pair, dza=1)
    q_far = ctx_send(q, dzb=2)
    near_pieces = [pair] + [ctx_send(pair, dy=bits) for bits in (1, 2, 3)]
    queries = [q, q_far, ctx_send(jnp.concatenate([q, q_far]), dzb=1)]
    parts = weight_parts(place, out_weight)
    weights = [parts[0]] + [head_send(parts[bits], dx=bits) for bits in (1, 2, 3)]
    far_pieces = [far] + [ctx_send(far, dy=bits) for bits in (1, 2, 3)]

    expo_near, stats_near = first_scores(queries, near_pieces)
    far_pieces, weights, stats_near = lax.optimization_barrier((far_pieces, weights, stats_near))
    expo_far, stats_far, stats = second_scores(place, queries, far_pieces, stats_near)
    expos = (expo_near, expo_far)
    factor, sums = columns(place, expos, (stats_near, stats_far), swap(stats, "ctx", LINE))
    attended = attend(place, expos, factor, near_pieces + far_pieces, swap(sums, "ctx", PLANE))
    whole = jnp.sum(swap(attended, "ctx", LINE).astype(F32), axis=0).astype(BF16)
    rows = swap(jnp.broadcast_to(whole, (4, ROWS, DIM)), "head", ROW)
    keep, send = project(place, rows, weights)
    both = keep + head_send(send, dcore=1)
    far = head_send(both[:, 128:].astype(BF16), dzh=1)
    return (both[:, :128] + far.astype(F32)).astype(BF16)


def solution(mesh):
    placed = (
        P("ctx", "head", None),
        P("ctx", "head", None),
        P("ctx", "head", None),
        P("head", None),
    )
    return jax.shard_map(
        shards, mesh=mesh, in_specs=placed, out_specs=P("ctx", "head"), check_vma=False
    )
```

time: 1200 us -> 148 us (0.12)
  the two profiles are of different devices: /device:TPU:8 before, /device:TPU:33 now
where the time goes in v1:
time: 148 us; the launch traced here: 147 us
  starting transfers between devices  62.3 us (42%)
  blocking collectives  49.8 us (34%)
  Pallas kernels  16.8 us (11%)
  waiting for transfers between devices  13.1 us (9%)
  other arithmetic  2.65 us (2%)
  local copies, waits for them, and re-layouts  2.08 us (1%)
    all_to_all x4, blocking collectives, swap(): lax.all_to_all(value, axis, 0, 0, axis_index_groups=groups, tiled=True)  49.8 us
    ppermute x9, starting transfers between devices, ctx_send(): return lax.ppermute(value, 'ctx', [(i, i ^ step) for i in range(32)])  33.7 us
    ppermute x5, starting transfers between devices, head_send(): return lax.ppermute(value, 'head', [(i, i ^ step) for i in range(16)])  28.6 us
    ppermute x5, waiting for transfers between devices, head_send(): return lax.ppermute(value, 'head', [(i, i ^ step) for i in range(16)])  12.8 us
    pallas_call x1, Pallas kernels, second_scores(): pl.pallas_call(second_score_kernel, in_specs=[SMEM] + [VMEM] * 8, out_spe...  4.44 us
    pallas_call x1, Pallas kernels, attend(): pl.pallas_call(value_kernel, grid=(QB,), in_specs=[SMEM, EXPO, EXPO] + [V...  4.41 us
    pallas_call x1, Pallas kernels, first_scores(): pl.pallas_call(first_score_kernel, in_specs=[VMEM] * 7, out_specs=[EXPO,...  3.8 us
  transfers between devices with their start and end apart: 14, of which 4 were waited for; matrix products, arithmetic and copies ran while one was open for 1% of the time, Pallas kernels for 3%

profile of v1, /device:TPU:33, one launch (start us, length us, event | category | flops | bytes accessed | tf_op | source)
XLA Modules:
  0.0 146.9 jit_solution(10903701789002613542)
XLA Ops:
  0.0 1.0 pad_maximum_fusion.refs_3_.refs_0_
  1.0 4.9 %collective-permute-start = (bf16[1,384,128]{2,1,0:T(8,128)(2,1)}, bf16[1,384,128]{2,1,0:T(8,128)(2,1)S(1)}, u32[]{:S(2)}, u32[]{:S(2)}) collective-permute-start(bf16[1,384,128]{2,1,0:T(8,128)(2,1)} %bitcast.8), channel_id=1, source_target_pairs={{0,32},{16,48},{32,0},{48,16},{64,96},{80,112},{96,64},{112,80},{1... | collective-permute-start | bytes 294920 | tf_op jit(solution)/shard_map/ppermute | solution.py:30
  5.9 0.1 stack.23.place_ref
  6.0 1.0 copy-done.1
  7.1 0.7 shard_map.47
  7.7 3.1 %collective-permute-start.9 = (bf16[128,512]{1,0:T(8,128)(2,1)S(1)}, bf16[128,512]{1,0:T(8,128)(2,1)S(1)}, u32[]{:S(2)}, u32[]{:S(2)}) collective-permute-start(bf16[128,512]{1,0:T(8,128)(2,1)S(1)} %get-tuple-element.35), channel_id=1, source_target_pairs={{0,2},{1,3},{2,0},{3,1},{4,6},{5,7},{6,4},{7,5},{8,10},{9,11},{10,... | collective-permute-start | bytes 393224 | tf_op jit(solution)/shard_map/ppermute | solution.py:35
  10.9 8.8 %collective-permute-start.5 = (bf16[2,384,128]{2,1,0:T(8,128)(2,1)S(1)}, bf16[2,384,128]{2,1,0:T(8,128)(2,1)S(1)}, u32[]{:S(2)}, u32[]{:S(2)}) collective-permute-start(bf16[2,384,128]{2,1,0:T(8,128)(2,1)S(1)} %pad_maximum_fusion.refs_3_.refs_0_), channel_id=1, source_target_pairs={{0,64},{16,80},{32,96},{48,112},{64,0},{80,16},{96,32},{112,48},{1... | collective-permute-start | bytes 589832 | tf_op jit(solution)/shard_map/ppermute | solution.py:30
  19.7 4.6 %collective-permute-start.4 = (bf16[2,384,128]{2,1,0:T(8,128)(2,1)S(1)}, bf16[2,384,128]{2,1,0:T(8,128)(2,1)S(1)}, u32[]{:S(2)}, u32[]{:S(2)}) collective-permute-start(bf16[2,384,128]{2,1,0:T(8,128)(2,1)S(1)} %pad_maximum_fusion.refs_3_.refs_0_), channel_id=1, source_target_pairs={{0,384},{16,400},{32,416},{48,432},{64,448},{80,464},{96,480},{112... | collective-permute-start | bytes 589832 | tf_op jit(solution)/shard_map/ppermute | solution.py:30
  24.4 2.3 %collective-permute-start.3 = (bf16[2,384,128]{2,1,0:T(8,128)(2,1)S(1)}, bf16[2,384,128]{2,1,0:T(8,128)(2,1)S(1)}, u32[]{:S(2)}, u32[]{:S(2)}) collective-permute-start(bf16[2,384,128]{2,1,0:T(8,128)(2,1)S(1)} %pad_maximum_fusion.refs_3_.refs_0_), channel_id=1, source_target_pairs={{0,256},{16,272},{32,288},{48,304},{64,320},{80,336},{96,352},{112... | collective-permute-start | bytes 589832 | tf_op jit(solution)/shard_map/ppermute | solution.py:30
  26.6 0.0 collective-permute-done.refs_1_
  26.6 2.1 %collective-permute-start.2 = (bf16[2,384,128]{2,1,0:T(8,128)(2,1)S(1)}, bf16[2,384,128]{2,1,0:T(8,128)(2,1)S(1)}, u32[]{:S(2)}, u32[]{:S(2)}) collective-permute-start(bf16[2,384,128]{2,1,0:T(8,128)(2,1)S(1)} %pad_maximum_fusion.refs_3_.refs_0_), channel_id=1, source_target_pairs={{0,128},{16,144},{32,160},{48,176},{64,192},{80,208},{96,224},{112... | collective-permute-start | bytes 589832 | tf_op jit(solution)/shard_map/ppermute | solution.py:30
  28.8 0.9 pad_maximum_fusion.1
  29.7 0.0 collective-permute-done.9.refs_1_
  29.7 1.9 %collective-permute-start.1 = (bf16[2,384,128]{2,1,0:T(8,128)(2,1)S(1)}, bf16[2,384,128]{2,1,0:T(8,128)(2,1)S(1)}, u32[]{:S(2)}, u32[]{:S(2)}) collective-permute-start(bf16[2,384,128]{2,1,0:T(8,128)(2,1)S(1)} %pad_maximum_fusion.1), channel_id=1, source_target_pairs={{0,16},{16,0},{32,48},{48,32},{64,80},{80,64},{96,112},{112,96},{1... | collective-permute-start | bytes 589832 | tf_op jit(solution)/shard_map/ppermute | solution.py:30
  31.6 0.3 collective-permute-done.5.refs_3_.refs_4_
  31.9 4.6 %collective-permute-start.8 = (bf16[2,384,128]{2,1,0:T(8,128)(2,1)S(1)}, bf16[2,384,128]{2,1,0:T(8,128)(2,1)S(1)}, u32[]{:S(2)}, u32[]{:S(2)}) collective-permute-start(bf16[2,384,128]{2,1,0:T(8,128)(2,1)S(1)} %collective-permute-done.5.refs_3_.refs_4_), channel_id=1, source_target_pairs={{0,384},{16,400},{32,416},{48,432},{64,448},{80,464},{96,480},{112... | collective-permute-start | bytes 589832 | tf_op jit(solution)/shard_map/ppermute | solution.py:30
  36.5 0.0 collective-permute-done.4.refs_6_.refs_3_
  36.5 2.3 %collective-permute-start.7 = (bf16[2,384,128]{2,1,0:T(8,128)(2,1)S(1)}, bf16[2,384,128]{2,1,0:T(8,128)(2,1)S(1)}, u32[]{:S(2)}, u32[]{:S(2)}) collective-permute-start(bf16[2,384,128]{2,1,0:T(8,128)(2,1)S(1)} %collective-permute-done.5.refs_3_.refs_4_), channel_id=1, source_target_pairs={{0,256},{16,272},{32,288},{48,304},{64,320},{80,336},{96,352},{112... | collective-permute-start | bytes 589832 | tf_op jit(solution)/shard_map/ppermute | solution.py:30
  38.8 0.0 collective-permute-done.3.refs_5_.refs_2_
  38.8 2.1 %collective-permute-start.6 = (bf16[2,384,128]{2,1,0:T(8,128)(2,1)S(1)}, bf16[2,384,128]{2,1,0:T(8,128)(2,1)S(1)}, u32[]{:S(2)}, u32[]{:S(2)}) collective-permute-start(bf16[2,384,128]{2,1,0:T(8,128)(2,1)S(1)} %collective-permute-done.5.refs_3_.refs_4_), channel_id=1, source_target_pairs={{0,128},{16,144},{32,160},{48,176},{64,192},{80,208},{96,224},{112... | collective-permute-start | bytes 589832 | tf_op jit(solution)/shard_map/ppermute | solution.py:30
  41.0 0.0 collective-permute-done.2.refs_4_.refs_1_
  41.0 4.4 %collective-permute-start.10 = (bf16[128,512]{1,0:T(8,128)(2,1)S(1)}, bf16[128,512]{1,0:T(8,128)(2,1)S(1)}, u32[]{:S(2)}, u32[]{:S(2)}) collective-permute-start(bf16[128,512]{1,0:T(8,128)(2,1)S(1)} %get-tuple-element.36), channel_id=1, source_target_pairs={{0,4},{1,5},{2,6},{3,7},{4,0},{5,1},{6,2},{7,3},{8,12},{9,13},{10,... | collective-permute-start | bytes 393224 | tf_op jit(solution)/shard_map/ppermute | solution.py:35
  45.4 0.0 collective-permute-done.1.refs_2_
  45.4 2.1 %collective-permute-start.11 = (bf16[128,512]{1,0:T(8,128)(2,1)S(1)}, bf16[128,512]{1,0:T(8,128)(2,1)S(1)}, u32[]{:S(2)}, u32[]{:S(2)}) collective-permute-start(bf16[128,512]{1,0:T(8,128)(2,1)S(1)} %get-tuple-element.37), channel_id=1, source_target_pairs={{0,6},{1,7},{2,4},{3,5},{4,2},{5,3},{6,0},{7,1},{8,14},{9,15},{10,... | collective-permute-start | bytes 393224 | tf_op jit(solution)/shard_map/ppermute | solution.py:35
  47.5 0.0 copy-start
  47.5 0.9 copy-done
  48.4 3.8 %shard_map.46 = (bf16[1536,1536]{1,0:T(8,128)(2,1)S(1)}, f32[4,8,128]{2,1,0:T(8,128)S(1)}) custom-call(bf16[1,384,128]{2,1,0:T(8,128)(2,1)S(1)} %bitcast.10, bf16[1,384,128]{2,1,0:T(8,128)(2,1)S(1)} %collective-permute-done.refs_1_, bf16[2,384,128]{2,1,0:T(8,128)(2,1)S(1)} %collective-permute-done.1.refs_2_, ...), custom_call_target="tpu_custom_call" | custom-call | tf_op jit(solution)/shard_map/pallas_call | solution.py:128
  52.2 0.0 collective-permute-done.10.refs_2_
  52.2 0.8 collective-permute-done.11.refs_3_
  53.0 0.0 collective-permute-done.8.refs_6_.refs_7_
  53.0 0.0 collective-permute-done.7.refs_5_.refs_6_
  53.0 0.0 collective-permute-done.6.refs_4_.refs_5_
  53.0 4.4 %shard_map.48 = (bf16[1536,1536]{1,0:T(8,128)(2,1)S(1)}, f32[4,8,128]{2,1,0:T(8,128)S(1)}, f32[4,4,8,128]{3,2,1,0:T(8,128)S(1)}) custom-call(s32[5]{0:T(128)S(1)} %stack.23.place_ref, bf16[1,384,128]{2,1,0:T(8,128)(2,1)S(1)} %bitcast.11, bf16[1,384,128]{2,1,0:T(8,128)(2,1)S(1)} %collective-permute-done.refs_1_, ...), custom_call_target="tpu_custom_call" | custom-call | tf_op jit(solution)/shard_map/pallas_call | solution.py:138
  57.4 10.8 %all_to_all.20.all_ref = f32[4,4,8,128]{3,2,1,0:T(8,128)S(1)} all-to-all(f32[4,4,8,128]{3,2,1,0:T(8,128)S(1)} %get-tuple-element.46), channel_id=1, replica_groups={{0,16,32,48},{64,80,96,112},{128,144,160,176},{192,208,224,240},{256,27..., dimensions={0} | all-to-all | bytes 131072 | tf_op jit(solution)/shard_map/all_to_all | solution.py:44
  68.3 2.3 %shard_map.49 = (f32[2,4,8,128]{3,2,1,0:T(8,128)S(1)}, f32[8,8,384]{2,1,0:T(8,128)S(1)}) custom-call(s32[5]{0:T(128)S(1)} %stack.23.place_ref, bf16[1536,1536]{1,0:T(8,128)(2,1)S(1)} %get-tuple-element.32.e0_ref, bf16[1536,1536]{1,0:T(8,128)(2,1)S(1)} %get-tuple-element.44.e1_ref, f32[4,8,128]{2,1,0:T(8,128)S(1)} %get-tuple-element.43.refs_7_.stat0_ref, ...), custom_call_target="tpu_custom_call" | custom-call | tf_op jit(solution)/shard_map/pallas_call | solution.py:186
  70.6 19.2 %all_to_all.21.refs_8_ = f32[8,8,384]{2,1,0:T(8,128)S(1)} all-to-all(f32[8,8,384]{2,1,0:T(8,128)S(1)} %get-tuple-element.48), channel_id=1, replica_groups={{0,64,128,192,256,320,384,448},{16,80,144,208,272,336,400,464},{32,96,1..., dimensions={0} | all-to-all | bytes 196608 | tf_op jit(solution)/shard_map/all_to_all | solution.py:44
  89.8 4.4 %shard_map.50 = bf16[4,384,128]{2,1,0:T(8,128)(2,1)S(1)} custom-call(s32[5]{0:T(128)S(1)} %stack.23.place_ref, bf16[1536,1536]{1,0:T(8,128)(2,1)S(1)} %get-tuple-element.32.e0_ref, bf16[1536,1536]{1,0:T(8,128)(2,1)S(1)} %get-tuple-element.44.e1_ref, f32[2,4,8,128]{3,2,1,0:T(8,128)S(1)} %get-tuple-element.47.factor_ref, ...), custom_call_target="tpu_custom_call" | custom-call | tf_op jit(solution)/shard_map/pallas_call | solution.py:236
  94.2 10.1 %all_to_all.22 = bf16[4,384,128]{2,1,0:T(8,128)(2,1)S(1)} all-to-all(bf16[4,384,128]{2,1,0:T(8,128)(2,1)S(1)} %shard_map.50), channel_id=1, replica_groups={{0,16,32,48},{64,80,96,112},{128,144,160,176},{192,208,224,240},{256,27..., dimensions={0} | all-to-all | bytes 786432 | tf_op jit(solution)/shard_map/all_to_all | solution.py:44
  104.3 0.1 reduce_sum.12
  104.4 0.1 broadcast_in_dim.3
  104.4 9.7 %all_to_all.23.rows_ref = bf16[4,384,128]{2,1,0:T(8,128)(2,1)S(1)} all-to-all(bf16[4,384,128]{2,1,0:T(8,128)(2,1)S(1)} %broadcast_in_dim.3), channel_id=1, replica_groups={{0,2,4,6},{1,3,5,7},{8,10,12,14},{9,11,13,15},{16,18,20,22},{17,19,21,2..., dimensions={0} | all-to-all | bytes 786432 | tf_op jit(solution)/shard_map/all_to_all | solution.py:44
  114.1 1.1 shard_map.51
  115.2 9.3 %collective-permute-start.12 = (f32[384,256]{1,0:T(8,128)S(1)}, f32[384,256]{1,0:T(8,128)S(1)}, u32[]{:S(2)}, u32[]{:S(2)}) collective-permute-start(f32[384,256]{1,0:T(8,128)S(1)} %get-tuple-element.54), channel_id=1, source_target_pairs={{0,1},{1,0},{2,3},{3,2},{4,5},{5,4},{6,7},{7,6},{8,9},{9,8},{10,11... | collective-permute-start | bytes 1179656 | tf_op jit(solution)/shard_map/ppermute | solution.py:35
  124.5 1.3 collective-permute-done.12
  125.8 0.1 add.22
  125.9 9.7 %collective-permute-start.13 = (bf16[384,128]{1,0:T(8,128)(2,1)S(1)}, bf16[384,128]{1,0:T(8,128)(2,1)S(1)}, u32[]{:S(2)}, u32[]{:S(2)}) collective-permute-start(bf16[384,128]{1,0:T(8,128)(2,1)S(1)} %slice.15), channel_id=1, source_target_pairs={{0,8},{1,9},{2,10},{3,11},{4,12},{5,13},{6,14},{7,15},{8,0},{9,1},... | collective-permute-start | bytes 294920 | tf_op jit(solution)/shard_map/ppermute | solution.py:35
  135.6 10.7 %collective-permute-done.13 = bf16[384,128]{1,0:T(8,128)(2,1)S(1)} collective-permute-done((bf16[384,128]{1,0:T(8,128)(2,1)S(1)}, bf16[384,128]{1,0:T(8,128)(2,1)S(1)}, u32[]{:S(2)}, u32[]{:S(2)}) %collective-permute-start.13) | collective-permute-done | bytes 98336 | tf_op jit(solution)/shard_map/ppermute | solution.py:35
  146.3 0.7 fusion
  (2 shorter events, 0.0 us)
Async XLA Ops:
  1.0 25.7 %collective-permute-start = (bf16[1,384,128]{2,1,0:T(8,128)(2,1)}, bf16[1,384,128]{2,1,0:T(8,128)(2,1)S(1)}, u32[]{:S(2)}, u32[]{:S(2)}) collective-permute-start(bf16[1,384,128]{2,1,0:T(8,128)(2,1)} %bitcast.8), channel_id=1, source_target_pairs={{0,32},{16,48},{32,0},{48,16},{64,96},{80,112},{96,64},{112,80},{1... | collective-permute-start | bytes 294920 | tf_op jit(solution)/shard_map/ppermute | solution.py:30
  6.0 1.0 copy-start.1
  7.7 22.0 %collective-permute-start.9 = (bf16[128,512]{1,0:T(8,128)(2,1)S(1)}, bf16[128,512]{1,0:T(8,128)(2,1)S(1)}, u32[]{:S(2)}, u32[]{:S(2)}) collective-permute-start(bf16[128,512]{1,0:T(8,128)(2,1)S(1)} %get-tuple-element.35), channel_id=1, source_target_pairs={{0,2},{1,3},{2,0},{3,1},{4,6},{5,7},{6,4},{7,5},{8,10},{9,11},{10,... | collective-permute-start | bytes 393224 | tf_op jit(solution)/shard_map/ppermute | solution.py:35
  10.9 21.0 %collective-permute-start.5 = (bf16[2,384,128]{2,1,0:T(8,128)(2,1)S(1)}, bf16[2,384,128]{2,1,0:T(8,128)(2,1)S(1)}, u32[]{:S(2)}, u32[]{:S(2)}) collective-permute-start(bf16[2,384,128]{2,1,0:T(8,128)(2,1)S(1)} %pad_maximum_fusion.refs_3_.refs_0_), channel_id=1, source_target_pairs={{0,64},{16,80},{32,96},{48,112},{64,0},{80,16},{96,32},{112,48},{1... | collective-permute-start | bytes 589832 | tf_op jit(solution)/shard_map/ppermute | solution.py:30
  19.7 16.8 %collective-permute-start.4 = (bf16[2,384,128]{2,1,0:T(8,128)(2,1)S(1)}, bf16[2,384,128]{2,1,0:T(8,128)(2,1)S(1)}, u32[]{:S(2)}, u32[]{:S(2)}) collective-permute-start(bf16[2,384,128]{2,1,0:T(8,128)(2,1)S(1)} %pad_maximum_fusion.refs_3_.refs_0_), channel_id=1, source_target_pairs={{0,384},{16,400},{32,416},{48,432},{64,448},{80,464},{96,480},{112... | collective-permute-start | bytes 589832 | tf_op jit(solution)/shard_map/ppermute | solution.py:30
  24.4 14.5 %collective-permute-start.3 = (bf16[2,384,128]{2,1,0:T(8,128)(2,1)S(1)}, bf16[2,384,128]{2,1,0:T(8,128)(2,1)S(1)}, u32[]{:S(2)}, u32[]{:S(2)}) collective-permute-start(bf16[2,384,128]{2,1,0:T(8,128)(2,1)S(1)} %pad_maximum_fusion.refs_3_.refs_0_), channel_id=1, source_target_pairs={{0,256},{16,272},{32,288},{48,304},{64,320},{80,336},{96,352},{112... | collective-permute-start | bytes 589832 | tf_op jit(solution)/shard_map/ppermute | solution.py:30
  26.6 14.3 %collective-permute-start.2 = (bf16[2,384,128]{2,1,0:T(8,128)(2,1)S(1)}, bf16[2,384,128]{2,1,0:T(8,128)(2,1)S(1)}, u32[]{:S(2)}, u32[]{:S(2)}) collective-permute-start(bf16[2,384,128]{2,1,0:T(8,128)(2,1)S(1)} %pad_maximum_fusion.refs_3_.refs_0_), channel_id=1, source_target_pairs={{0,128},{16,144},{32,160},{48,176},{64,192},{80,208},{96,224},{112... | collective-permute-start | bytes 589832 | tf_op jit(solution)/shard_map/ppermute | solution.py:30
  29.7 15.6 %collective-permute-start.1 = (bf16[2,384,128]{2,1,0:T(8,128)(2,1)S(1)}, bf16[2,384,128]{2,1,0:T(8,128)(2,1)S(1)}, u32[]{:S(2)}, u32[]{:S(2)}) collective-permute-start(bf16[2,384,128]{2,1,0:T(8,128)(2,1)S(1)} %pad_maximum_fusion.1), channel_id=1, source_target_pairs={{0,16},{16,0},{32,48},{48,32},{64,80},{80,64},{96,112},{112,96},{1... | collective-permute-start | bytes 589832 | tf_op jit(solution)/shard_map/ppermute | solution.py:30
  31.9 21.1 %collective-permute-start.8 = (bf16[2,384,128]{2,1,0:T(8,128)(2,1)S(1)}, bf16[2,384,128]{2,1,0:T(8,128)(2,1)S(1)}, u32[]{:S(2)}, u32[]{:S(2)}) collective-permute-start(bf16[2,384,128]{2,1,0:T(8,128)(2,1)S(1)} %collective-permute-done.5.refs_3_.refs_4_), channel_id=1, source_target_pairs={{0,384},{16,400},{32,416},{48,432},{64,448},{80,464},{96,480},{112... | collective-permute-start | bytes 589832 | tf_op jit(solution)/shard_map/ppermute | solution.py:30
  36.5 16.5 %collective-permute-start.7 = (bf16[2,384,128]{2,1,0:T(8,128)(2,1)S(1)}, bf16[2,384,128]{2,1,0:T(8,128)(2,1)S(1)}, u32[]{:S(2)}, u32[]{:S(2)}) collective-permute-start(bf16[2,384,128]{2,1,0:T(8,128)(2,1)S(1)} %collective-permute-done.5.refs_3_.refs_4_), channel_id=1, source_target_pairs={{0,256},{16,272},{32,288},{48,304},{64,320},{80,336},{96,352},{112... | collective-permute-start | bytes 589832 | tf_op jit(solution)/shard_map/ppermute | solution.py:30
  38.8 14.2 %collective-permute-start.6 = (bf16[2,384,128]{2,1,0:T(8,128)(2,1)S(1)}, bf16[2,384,128]{2,1,0:T(8,128)(2,1)S(1)}, u32[]{:S(2)}, u32[]{:S(2)}) collective-permute-start(bf16[2,384,128]{2,1,0:T(8,128)(2,1)S(1)} %collective-permute-done.5.refs_3_.refs_4_), channel_id=1, source_target_pairs={{0,128},{16,144},{32,160},{48,176},{64,192},{80,208},{96,224},{112... | collective-permute-start | bytes 589832 | tf_op jit(solution)/shard_map/ppermute | solution.py:30
  41.0 11.2 %collective-permute-start.10 = (bf16[128,512]{1,0:T(8,128)(2,1)S(1)}, bf16[128,512]{1,0:T(8,128)(2,1)S(1)}, u32[]{:S(2)}, u32[]{:S(2)}) collective-permute-start(bf16[128,512]{1,0:T(8,128)(2,1)S(1)} %get-tuple-element.36), channel_id=1, source_target_pairs={{0,4},{1,5},{2,6},{3,7},{4,0},{5,1},{6,2},{7,3},{8,12},{9,13},{10,... | collective-permute-start | bytes 393224 | tf_op jit(solution)/shard_map/ppermute | solution.py:35
  45.4 7.6 %collective-permute-start.11 = (bf16[128,512]{1,0:T(8,128)(2,1)S(1)}, bf16[128,512]{1,0:T(8,128)(2,1)S(1)}, u32[]{:S(2)}, u32[]{:S(2)}) collective-permute-start(bf16[128,512]{1,0:T(8,128)(2,1)S(1)} %get-tuple-element.37), channel_id=1, source_target_pairs={{0,6},{1,7},{2,4},{3,5},{4,2},{5,3},{6,0},{7,1},{8,14},{9,15},{10,... | collective-permute-start | bytes 393224 | tf_op jit(solution)/shard_map/ppermute | solution.py:35
  47.5 0.9 copy-start
  115.2 10.6 %collective-permute-start.12 = (f32[384,256]{1,0:T(8,128)S(1)}, f32[384,256]{1,0:T(8,128)S(1)}, u32[]{:S(2)}, u32[]{:S(2)}) collective-permute-start(f32[384,256]{1,0:T(8,128)S(1)} %get-tuple-element.54), channel_id=1, source_target_pairs={{0,1},{1,0},{2,3},{3,2},{4,5},{5,4},{6,7},{7,6},{8,9},{9,8},{10,11... | collective-permute-start | bytes 1179656 | tf_op jit(solution)/shard_map/ppermute | solution.py:35
  125.9 20.4 %collective-permute-start.13 = (bf16[384,128]{1,0:T(8,128)(2,1)S(1)}, bf16[384,128]{1,0:T(8,128)(2,1)S(1)}, u32[]{:S(2)}, u32[]{:S(2)}) collective-permute-start(bf16[384,128]{1,0:T(8,128)(2,1)S(1)} %slice.15), channel_id=1, source_target_pairs={{0,8},{1,9},{2,10},{3,11},{4,12},{5,13},{6,14},{7,15},{8,0},{9,1},... | collective-permute-start | bytes 294920 | tf_op jit(solution)/shard_map/ppermute | solution.py:35

commit v2 on v1

--- a/solution.py
+++ b/solution.py
@@ -59,10 +59,8 @@
 def gather_queries(u, q_refs, q_all):
     @pl.when(u == 0)
     def _():
-        q_all[0] = q_refs[0][0]
-        q_all[1] = q_refs[1][0]
-        q_all[2] = q_refs[2][0]
-        q_all[3] = q_refs[2][1]
+        for at in range(QB):
+            q_all[at] = q_refs[at // 2][at % 2]
 
 
 def half_scores(u, q_all, kv_refs, e_ref, s_ref):
@@ -87,7 +85,7 @@
 
 
 def first_score_kernel(*refs):
-    q_refs, kv_refs, (e_ref, stat_ref, q_all, s_ref) = refs[:3], refs[3:7], refs[7:]
+    q_refs, kv_refs, (e_ref, stat_ref, q_all, s_ref) = refs[:2], refs[2:6], refs[6:]
     u = pl.program_id(0)
     gather_queries(u, q_refs, q_all)
     stat_ref[u] = half_scores(u, q_all, kv_refs, e_ref, s_ref)
@@ -101,8 +99,8 @@
 
 
 def second_score_kernel(place_ref, *refs):
-    q_refs, kv_refs, first_ref = refs[:3], refs[3:7], refs[7]
-    e_ref, stat_ref, both_ref, q_all, s_ref = refs[8:]
+    q_refs, kv_refs, first_ref = refs[:2], refs[2:6], refs[6]
+    e_ref, stat_ref, both_ref, q_all, s_ref = refs[7:]
     u = pl.program_id(0)
     gather_queries(u, q_refs, q_all)
     rows = half_scores(u, q_all, kv_refs, e_ref, s_ref)
@@ -127,7 +125,7 @@
 def first_scores(queries, pieces):
     return pl.pallas_call(
         first_score_kernel,
-        in_specs=[VMEM] * 7,
+        in_specs=[VMEM] * 6,
         out_specs=[EXPO, VMEM],
         out_shape=[EXPO_TYPE, STAT_TYPE],
         **SCORE,
@@ -137,7 +135,7 @@
 def second_scores(place, queries, pieces, stats):
     return pl.pallas_call(
         second_score_kernel,
-        in_specs=[SMEM] + [VMEM] * 8,
+        in_specs=[SMEM] + [VMEM] * 7,
         out_specs=[EXPO, VMEM, VMEM],
         out_shape=[EXPO_TYPE, STAT_TYPE, jax.ShapeDtypeStruct((QB, QB, 8, 128), F32)],
         **SCORE,
@@ -244,47 +242,47 @@
     )(place, *expos, factor, *pieces, sums)
 
 
-def weight_kernel(place_ref, w_ref, *outs):
-    zh, x, core = place_ref[2], place_ref[3], place_ref[4]
-    for dx in range(4):
-        for dcore in range(2):
-            for dzh in range(2):
-                to = (zh ^ dzh) * 8 + (x ^ dx) * 2 + (core ^ dcore)
-                at = dcore * 2 + dzh
-                outs[dx][:, at * 128 : (at + 1) * 128] = w_ref[
-                    :, pl.ds(pl.multiple_of(to * 128, 128), 128)
-                ]
-
-
-def weight_parts(place, out_weight):
-    return pl.pallas_call(
-        weight_kernel,
-        in_specs=[SMEM, VMEM],
-        out_specs=[VMEM] * 4,
-        out_shape=[jax.ShapeDtypeStruct((DIM, 512), BF16)] * 4,
+def project_kernel(place_ref, own_ref, other_ref, w0_ref, w1_ref, out_ref, w_ref):
+    zh, core = place_ref[2], place_ref[4]
+    for x in range(4):
+        for dzh in range(2):
+            head = (zh ^ dzh) * 8 + x * 2 + core
+            lanes = pl.ds(pl.multiple_of(head * 128, 128), 128)
+            at = slice((x * 2 + dzh) * 128, (x * 2 + dzh + 1) * 128)
+            w_ref[:DIM, at] = w0_ref[:, lanes]
+            w_ref[DIM:, at] = w1_ref[:, lanes]
+    rows = jnp.concatenate([own_ref[...], other_ref[...]], axis=1)
+    for x in range(4):
+        out_ref[x] = jnp.dot(
+            rows, w_ref[:, x * 256 : (x + 1) * 256], preferred_element_type=F32
+        ).astype(BF16)
+
+
+def project(place, own, other, w_own, w_other):
+    return pl.pallas_call(
+        project_kernel,
+        in_specs=[SMEM] + [VMEM] * 4,
+        out_specs=VMEM,
+        out_shape=jax.ShapeDtypeStruct((4, ROWS, 256), BF16),
+        scratch_shapes=[pltpu.VMEM((2 * DIM, 1024), BF16)],
+        compiler_params=pltpu.CompilerParams(vmem_limit_bytes=16 * 1024 * 1024),
+    )(place, own, other, w_own, w_other)
+
+
+def query_pair_kernel(a_ref, b_ref, out_ref):
+    out_ref[0] = a_ref[0]
+    out_ref[1] = b_ref[0]
+
+
+def query_pair(a, b):
+    return pl.pallas_call(
+        query_pair_kernel,
+        in_specs=[VMEM] * 2,
+        out_specs=VMEM,
+        out_shape=jax.ShapeDtypeStruct((2, ROWS, DIM), BF16),
         compiler_params=pltpu.CompilerParams(vmem_limit_bytes=8 * 1024 * 1024),
-    )(place, out_weight)
-
-
-def project_kernel(place_ref, rows_ref, *refs):
-    weights, (keep_ref, send_ref) = refs[:4], refs[4:]
-    total = jnp.zeros((ROWS, 512), F32)
-    for bit in range(4):
-        total = total + jnp.dot(
-            rows_ref[place_ref[3] ^ bit], weights[bit][...], preferred_element_type=F32
-        )
-    keep_ref[...] = total[:, :256]
-    send_ref[...] = total[:, 256:]
-
-
-def project(place, rows, weights):
-    return pl.pallas_call(
-        project_kernel,
-        in_specs=[SMEM] + [VMEM] * 5,
-        out_specs=[VMEM] * 2,
-        out_shape=[jax.ShapeDtypeStruct((ROWS, 256), F32)] * 2,
-        compiler_params=pltpu.CompilerParams(vmem_limit_bytes=16 * 1024 * 1024),
-    )(place, rows, *weights)
+        cost_estimate=pl.CostEstimate(flops=2 * 10**10, bytes_accessed=10**6, transcendentals=0),
+    )(a, b)
 
 
 def shards(query_rows, key_rows, value_rows, out_weight):
@@ -293,25 +291,23 @@
     place = jnp.stack(
         [ctx % 4, ctx // 4, head // 8, head // 2 % 4, head % 2]
     ).astype(jnp.int32)
-    pair, q, out_weight = lax.optimization_barrier((jnp.concatenate([k, v]), q, out_weight))
+    pair, q = lax.optimization_barrier((jnp.concatenate([k, v]), q))
     far = ctx_send(pair, dza=1)
-    q_far = ctx_send(q, dzb=2)
+    q_two = query_pair(q, ctx_send(q, dzb=2))
     near_pieces = [pair] + [ctx_send(pair, dy=bits) for bits in (1, 2, 3)]
-    queries = [q, q_far, ctx_send(jnp.concatenate([q, q_far]), dzb=1)]
-    parts = weight_parts(place, out_weight)
-    weights = [parts[0]] + [head_send(parts[bits], dx=bits) for bits in (1, 2, 3)]
+    queries = [q_two, ctx_send(q_two, dzb=1)]
     far_pieces = [far] + [ctx_send(far, dy=bits) for bits in (1, 2, 3)]
 
     expo_near, stats_near = first_scores(queries, near_pieces)
-    far_pieces, weights, stats_near = lax.optimization_barrier((far_pieces, weights, stats_near))
+    w_other = head_send(out_weight, dcore=1)
+    far_pieces, w_other, stats_near = lax.optimization_barrier((far_pieces, w_other, stats_near))
     expo_far, stats_far, stats = second_scores(place, queries, far_pieces, stats_near)
     expos = (expo_near, expo_far)
     factor, sums = columns(place, expos, (stats_near, stats_far), swap(stats, "ctx", LINE))
     attended = attend(place, expos, factor, near_pieces + far_pieces, swap(sums, "ctx", PLANE))
     whole = jnp.sum(swap(attended, "ctx", LINE).astype(F32), axis=0).astype(BF16)
-    rows = swap(jnp.broadcast_to(whole, (4, ROWS, DIM)), "head", ROW)
-    keep, send = project(place, rows, weights)
-    both = keep + head_send(send, dcore=1)
+    parts = project(place, whole, head_send(whole, dcore=1), out_weight, w_other)
+    both = jnp.sum(swap(parts, "head", ROW).astype(F32), axis=0)
     far = head_send(both[:, 128:].astype(BF16), dzh=1)
     return (both[:, :128] + far.astype(F32)).astype(BF16)
 

time: 148 us -> 143 us (0.966)
  starting transfers between devices: 62.3 us -> 56.9 us
  waiting for transfers between devices: 13.1 us -> 15 us
  blocking collectives: 49.8 us -> 51.6 us
    ppermute x5 -> x3, starting transfers between devices: 28.6 us -> 20.4 us  [head_send(): return lax.ppermute(value, 'head', [(i, i ^ step) for i in range(16)])]
    ppermute x9, starting transfers between devices: 33.7 us -> 36.5 us  [ctx_send(): return lax.ppermute(value, 'ctx', [(i, i ^ step) for i in range(32)])]
    ppermute x9, waiting for transfers between devices: 0.27 us -> 2.72 us  [ctx_send(): return lax.ppermute(value, 'ctx', [(i, i ^ step) for i in range(32)])]
    all_to_all x4, blocking collectives: 49.8 us -> 51.6 us  [swap(): lax.all_to_all(value, axis, 0, 0, axis_index_groups=groups, tiled=True)]
    ppermute x5 -> x3, waiting for transfers between devices: 12.8 us -> 12.3 us  [head_send(): return lax.ppermute(value, 'head', [(i, i ^ step) for i in range(16)])]
  transfers between devices with their start and end apart: 14 -> 12, of which waited for: 4 -> 3; matrix products, arithmetic and copies ran while one was open for 1% -> 0% of each run, Pallas kernels for 3% -> 3%
where the time goes in v2:
time: 143 us
  starting transfers between devices  56.9 us (40%)
  blocking collectives  51.6 us (36%)
  Pallas kernels  16 us (11%)
  waiting for transfers between devices  15 us (10%)
  other arithmetic  1.79 us (1%)
    all_to_all x4, blocking collectives, swap(): lax.all_to_all(value, axis, 0, 0, axis_index_groups=groups, tiled=True)  51.6 us
    ppermute x9, starting transfers between devices, ctx_send(): return lax.ppermute(value, 'ctx', [(i, i ^ step) for i in range(32)])  36.5 us
    ppermute x3, starting transfers between devices, head_send(): return lax.ppermute(value, 'head', [(i, i ^ step) for i in range(16)])  20.4 us
    ppermute x3, waiting for transfers between devices, head_send(): return lax.ppermute(value, 'head', [(i, i ^ step) for i in range(16)])  12.3 us
    pallas_call x1, Pallas kernels, attend(): pl.pallas_call(value_kernel, grid=(QB,), in_specs=[SMEM, EXPO, EXPO] + [V...  4.4 us
    pallas_call x1, Pallas kernels, second_scores(): pl.pallas_call(second_score_kernel, in_specs=[SMEM] + [VMEM] * 7, out_spe...  4.4 us
    pallas_call x1, Pallas kernels, first_scores(): pl.pallas_call(first_score_kernel, in_specs=[VMEM] * 6, out_specs=[EXPO,...  3.79 us
  transfers between devices with their start and end apart: 12, of which 3 were waited for; matrix products, arithmetic and copies ran while one was open for 0% of the time, Pallas kernels for 3%

profile of v2, /device:TPU:33, one launch (start us, length us, event | category | flops | bytes accessed | tf_op | source)
XLA Modules:
  0.0 142.6 jit_solution(11341990130010058017)
XLA Ops:
  0.0 1.0 pad_maximum_fusion.refs_2_.refs_0_
  1.0 4.9 %collective-permute-start = (bf16[1,384,128]{2,1,0:T(8,128)(2,1)}, bf16[1,384,128]{2,1,0:T(8,128)(2,1)S(1)}, u32[]{:S(2)}, u32[]{:S(2)}) collective-permute-start(bf16[1,384,128]{2,1,0:T(8,128)(2,1)} %bitcast.8), channel_id=1, source_target_pairs={{0,32},{16,48},{32,0},{48,16},{64,96},{80,112},{96,64},{112,80},{1... | collective-permute-start | bytes 294920 | tf_op jit(solution)/shard_map/ppermute | solution.py:30
  5.9 8.8 %collective-permute-start.5 = (bf16[2,384,128]{2,1,0:T(8,128)(2,1)S(1)}, bf16[2,384,128]{2,1,0:T(8,128)(2,1)S(1)}, u32[]{:S(2)}, u32[]{:S(2)}) collective-permute-start(bf16[2,384,128]{2,1,0:T(8,128)(2,1)S(1)} %pad_maximum_fusion.refs_2_.refs_0_), channel_id=1, source_target_pairs={{0,64},{16,80},{32,96},{48,112},{64,0},{80,16},{96,32},{112,48},{1... | collective-permute-start | bytes 589832 | tf_op jit(solution)/shard_map/ppermute | solution.py:30
  14.7 4.6 %collective-permute-start.4 = (bf16[2,384,128]{2,1,0:T(8,128)(2,1)S(1)}, bf16[2,384,128]{2,1,0:T(8,128)(2,1)S(1)}, u32[]{:S(2)}, u32[]{:S(2)}) collective-permute-start(bf16[2,384,128]{2,1,0:T(8,128)(2,1)S(1)} %pad_maximum_fusion.refs_2_.refs_0_), channel_id=1, source_target_pairs={{0,384},{16,400},{32,416},{48,432},{64,448},{80,464},{96,480},{112... | collective-permute-start | bytes 589832 | tf_op jit(solution)/shard_map/ppermute | solution.py:30
  19.3 2.3 %collective-permute-start.3 = (bf16[2,384,128]{2,1,0:T(8,128)(2,1)S(1)}, bf16[2,384,128]{2,1,0:T(8,128)(2,1)S(1)}, u32[]{:S(2)}, u32[]{:S(2)}) collective-permute-start(bf16[2,384,128]{2,1,0:T(8,128)(2,1)S(1)} %pad_maximum_fusion.refs_2_.refs_0_), channel_id=1, source_target_pairs={{0,256},{16,272},{32,288},{48,304},{64,320},{80,336},{96,352},{112... | collective-permute-start | bytes 589832 | tf_op jit(solution)/shard_map/ppermute | solution.py:30
  21.6 2.1 %collective-permute-start.2 = (bf16[2,384,128]{2,1,0:T(8,128)(2,1)S(1)}, bf16[2,384,128]{2,1,0:T(8,128)(2,1)S(1)}, u32[]{:S(2)}, u32[]{:S(2)}) collective-permute-start(bf16[2,384,128]{2,1,0:T(8,128)(2,1)S(1)} %pad_maximum_fusion.refs_2_.refs_0_), channel_id=1, source_target_pairs={{0,128},{16,144},{32,160},{48,176},{64,192},{80,208},{96,224},{112... | collective-permute-start | bytes 589832 | tf_op jit(solution)/shard_map/ppermute | solution.py:30
  23.8 0.0 collective-permute-done.b_ref
  23.8 3.9 %collective-permute-start.9 = (bf16[128,2048]{1,0:T(8,128)(2,1)}, bf16[128,2048]{1,0:T(8,128)(2,1)S(1)}, u32[]{:S(2)}, u32[]{:S(2)}) collective-permute-start(bf16[128,2048]{1,0:T(8,128)(2,1)} %w0_ref.1), channel_id=1, source_target_pairs={{0,1},{1,0},{2,3},{3,2},{4,5},{5,4},{6,7},{7,6},{8,9},{9,8},{10,11... | collective-permute-start | bytes 1572872 | tf_op jit(solution)/shard_map/ppermute | solution.py:35
  27.7 0.0 copy-start.1
  27.7 0.9 copy-done.1
  28.6 0.0 collective-permute-done.5.refs_2_.refs_4_
  28.7 4.5 %collective-permute-start.1 = (bf16[2,384,128]{2,1,0:T(8,128)(2,1)S(1)}, bf16[2,384,128]{2,1,0:T(8,128)(2,1)S(1)}, u32[]{:S(2)}, u32[]{:S(2)}) collective-permute-start(bf16[2,384,128]{2,1,0:T(8,128)(2,1)S(1)} %shard_map.46.refs_0_), channel_id=1, source_target_pairs={{0,16},{16,0},{32,48},{48,32},{64,80},{80,64},{96,112},{112,96},{1... | collective-permute-start | bytes 589832 | tf_op jit(solution)/shard_map/ppermute | solution.py:30
  33.2 0.0 collective-permute-done.4.refs_5_.refs_3_
  33.2 4.8 %collective-permute-start.8 = (bf16[2,384,128]{2,1,0:T(8,128)(2,1)S(1)}, bf16[2,384,128]{2,1,0:T(8,128)(2,1)S(1)}, u32[]{:S(2)}, u32[]{:S(2)}) collective-permute-start(bf16[2,384,128]{2,1,0:T(8,128)(2,1)S(1)} %collective-permute-done.5.refs_2_.refs_4_), channel_id=1, source_target_pairs={{0,384},{16,400},{32,416},{48,432},{64,448},{80,464},{96,480},{112... | collective-permute-start | bytes 589832 | tf_op jit(solution)/shard_map/ppermute | solution.py:30
  38.0 0.0 collective-permute-done.3.refs_4_.refs_2_
  38.0 2.3 %collective-permute-start.7 = (bf16[2,384,128]{2,1,0:T(8,128)(2,1)S(1)}, bf16[2,384,128]{2,1,0:T(8,128)(2,1)S(1)}, u32[]{:S(2)}, u32[]{:S(2)}) collective-permute-start(bf16[2,384,128]{2,1,0:T(8,128)(2,1)S(1)} %collective-permute-done.5.refs_2_.refs_4_), channel_id=1, source_target_pairs={{0,256},{16,272},{32,288},{48,304},{64,320},{80,336},{96,352},{112... | collective-permute-start | bytes 589832 | tf_op jit(solution)/shard_map/ppermute | solution.py:30
  40.3 0.0 collective-permute-done.2.refs_3_.refs_1_
  40.3 2.1 %collective-permute-start.6 = (bf16[2,384,128]{2,1,0:T(8,128)(2,1)S(1)}, bf16[2,384,128]{2,1,0:T(8,128)(2,1)S(1)}, u32[]{:S(2)}, u32[]{:S(2)}) collective-permute-start(bf16[2,384,128]{2,1,0:T(8,128)(2,1)S(1)} %collective-permute-done.5.refs_2_.refs_4_), channel_id=1, source_target_pairs={{0,128},{16,144},{32,160},{48,176},{64,192},{80,208},{96,224},{112... | collective-permute-start | bytes 589832 | tf_op jit(solution)/shard_map/ppermute | solution.py:30
  42.5 0.1 stack.23.place_ref
  42.6 0.0 collective-permute-done.1.refs_1_
  42.6 3.8 %shard_map.47 = (bf16[1536,1536]{1,0:T(8,128)(2,1)S(1)}, f32[4,8,128]{2,1,0:T(8,128)S(1)}) custom-call(bf16[2,384,128]{2,1,0:T(8,128)(2,1)S(1)} %shard_map.46.refs_0_, bf16[2,384,128]{2,1,0:T(8,128)(2,1)S(1)} %collective-permute-done.1.refs_1_, bf16[2,384,128]{2,1,0:T(8,128)(2,1)S(1)} %pad_maximum_fusion.refs_2_.refs_0_, ...), custom_call_target="tpu_custom_call" | custom-call | tf_op jit(solution)/shard_map/pallas_call | solution.py:126
  46.4 0.0 collective-permute-done.8.refs_5_.refs_7_
  46.4 0.0 collective-permute-done.7.refs_4_.refs_6_
  46.4 2.7 %collective-permute-done.6.refs_3_.refs_5_ = bf16[2,384,128]{2,1,0:T(8,128)(2,1)S(1)} collective-permute-done((bf16[2,384,128]{2,1,0:T(8,128)(2,1)S(1)}, bf16[2,384,128]{2,1,0:T(8,128)(2,1)S(1)}, u32[]{:S(2)}, u32[]{:S(2)}) %collective-permute-start.6) | collective-permute-done | bytes 196640 | tf_op jit(solution)/shard_map/ppermute | solution.py:30
  49.1 0.0 collective-permute-done.9.w1_ref
  49.1 4.4 %shard_map.48 = (bf16[1536,1536]{1,0:T(8,128)(2,1)S(1)}, f32[4,8,128]{2,1,0:T(8,128)S(1)}, f32[4,4,8,128]{3,2,1,0:T(8,128)S(1)}) custom-call(s32[5]{0:T(128)S(1)} %stack.23.place_ref, bf16[2,384,128]{2,1,0:T(8,128)(2,1)S(1)} %shard_map.46.refs_0_, bf16[2,384,128]{2,1,0:T(8,128)(2,1)S(1)} %collective-permute-done.1.refs_1_, ...), custom_call_target="tpu_custom_call" | custom-call | tf_op jit(solution)/shard_map/pallas_call | solution.py:136
  53.5 6.4 %all_to_all.20.all_ref = f32[4,4,8,128]{3,2,1,0:T(8,128)S(1)} all-to-all(f32[4,4,8,128]{3,2,1,0:T(8,128)S(1)} %get-tuple-element.31), channel_id=1, replica_groups={{0,16,32,48},{64,80,96,112},{128,144,160,176},{192,208,224,240},{256,27..., dimensions={0} | all-to-all | bytes 131072 | tf_op jit(solution)/shard_map/all_to_all | solution.py:44
  59.9 2.3 %shard_map.49 = (f32[2,4,8,128]{3,2,1,0:T(8,128)S(1)}, f32[8,8,384]{2,1,0:T(8,128)S(1)}) custom-call(s32[5]{0:T(128)S(1)} %stack.23.place_ref, bf16[1536,1536]{1,0:T(8,128)(2,1)S(1)} %get-tuple-element.22.e0_ref, bf16[1536,1536]{1,0:T(8,128)(2,1)S(1)} %get-tuple-element.29.e1_ref, f32[4,8,128]{2,1,0:T(8,128)S(1)} %get-tuple-element.28.refs_6_.stat0_ref, ...), custom_call_target="tpu_custom_call" | custom-call | tf_op jit(solution)/shard_map/pallas_call | solution.py:184
  62.3 19.8 %all_to_all.21.refs_8_ = f32[8,8,384]{2,1,0:T(8,128)S(1)} all-to-all(f32[8,8,384]{2,1,0:T(8,128)S(1)} %get-tuple-element.33), channel_id=1, replica_groups={{0,64,128,192,256,320,384,448},{16,80,144,208,272,336,400,464},{32,96,1..., dimensions={0} | all-to-all | bytes 196608 | tf_op jit(solution)/shard_map/all_to_all | solution.py:44
  82.1 0.0 copy-start
  82.1 4.4 %shard_map.50 = bf16[4,384,128]{2,1,0:T(8,128)(2,1)S(1)} custom-call(s32[5]{0:T(128)S(1)} %stack.23.place_ref, bf16[1536,1536]{1,0:T(8,128)(2,1)S(1)} %get-tuple-element.22.e0_ref, bf16[1536,1536]{1,0:T(8,128)(2,1)S(1)} %get-tuple-element.29.e1_ref, f32[2,4,8,128]{3,2,1,0:T(8,128)S(1)} %get-tuple-element.32.factor_ref, ...), custom_call_target="tpu_custom_call" | custom-call | tf_op jit(solution)/shard_map/pallas_call | solution.py:234
  86.5 10.1 %all_to_all.22 = bf16[4,384,128]{2,1,0:T(8,128)(2,1)S(1)} all-to-all(bf16[4,384,128]{2,1,0:T(8,128)(2,1)S(1)} %shard_map.50), channel_id=1, replica_groups={{0,16,32,48},{64,80,96,112},{128,144,160,176},{192,208,224,240},{256,27..., dimensions={0} | all-to-all | bytes 786432 | tf_op jit(solution)/shard_map/all_to_all | solution.py:44
  96.6 0.1 reduce_sum.21.own_ref
  96.6 7.6 %collective-permute-start.10 = (bf16[384,128]{1,0:T(8,128)(2,1)S(1)}, bf16[384,128]{1,0:T(8,128)(2,1)S(1)}, u32[]{:S(2)}, u32[]{:S(2)}) collective-permute-start(bf16[384,128]{1,0:T(8,128)(2,1)S(1)} %reduce_sum.21.own_ref), channel_id=1, source_target_pairs={{0,1},{1,0},{2,3},{3,2},{4,5},{5,4},{6,7},{7,6},{8,9},{9,8},{10,11... | collective-permute-start | bytes 294920 | tf_op jit(solution)/shard_map/ppermute | solution.py:35
  104.2 0.9 collective-permute-done.10.other_ref
  105.1 0.0 copy-done
  105.1 1.1 shard_map.51
  106.2 15.3 %all_to_all.23 = bf16[4,384,256]{2,1,0:T(8,128)(2,1)S(1)} all-to-all(bf16[4,384,256]{2,1,0:T(8,128)(2,1)S(1)} %shard_map.51), channel_id=1, replica_groups={{0,2,4,6},{1,3,5,7},{8,10,12,14},{9,11,13,15},{16,18,20,22},{17,19,21,2..., dimensions={0} | all-to-all | bytes 1572864 | tf_op jit(solution)/shard_map/all_to_all | solution.py:44
  121.4 0.1 convert_reduce_fusion
  121.6 9.0 %collective-permute-start.11 = (bf16[384,128]{1,0:T(8,128)(2,1)S(1)}, bf16[384,128]{1,0:T(8,128)(2,1)S(1)}, u32[]{:S(2)}, u32[]{:S(2)}) collective-permute-start(bf16[384,128]{1,0:T(8,128)(2,1)S(1)} %slice.15), channel_id=1, source_target_pairs={{0,8},{1,9},{2,10},{3,11},{4,12},{5,13},{6,14},{7,15},{8,0},{9,1},... | collective-permute-start | bytes 294920 | tf_op jit(solution)/shard_map/ppermute | solution.py:35
  130.5 11.4 %collective-permute-done.11 = bf16[384,128]{1,0:T(8,128)(2,1)S(1)} collective-permute-done((bf16[384,128]{1,0:T(8,128)(2,1)S(1)}, bf16[384,128]{1,0:T(8,128)(2,1)S(1)}, u32[]{:S(2)}, u32[]{:S(2)}) %collective-permute-start.11) | collective-permute-done | bytes 98336 | tf_op jit(solution)/shard_map/ppermute | solution.py:35
  141.9 0.7 fusion
  (2 shorter events, 0.0 us)
Async XLA Ops:
  1.0 22.8 %collective-permute-start = (bf16[1,384,128]{2,1,0:T(8,128)(2,1)}, bf16[1,384,128]{2,1,0:T(8,128)(2,1)S(1)}, u32[]{:S(2)}, u32[]{:S(2)}) collective-permute-start(bf16[1,384,128]{2,1,0:T(8,128)(2,1)} %bitcast.8), channel_id=1, source_target_pairs={{0,32},{16,48},{32,0},{48,16},{64,96},{80,112},{96,64},{112,80},{1... | collective-permute-start | bytes 294920 | tf_op jit(solution)/shard_map/ppermute | solution.py:30
  5.9 22.8 %collective-permute-start.5 = (bf16[2,384,128]{2,1,0:T(8,128)(2,1)S(1)}, bf16[2,384,128]{2,1,0:T(8,128)(2,1)S(1)}, u32[]{:S(2)}, u32[]{:S(2)}) collective-permute-start(bf16[2,384,128]{2,1,0:T(8,128)(2,1)S(1)} %pad_maximum_fusion.refs_2_.refs_0_), channel_id=1, source_target_pairs={{0,64},{16,80},{32,96},{48,112},{64,0},{80,16},{96,32},{112,48},{1... | collective-permute-start | bytes 589832 | tf_op jit(solution)/shard_map/ppermute | solution.py:30
  14.7 18.5 %collective-permute-start.4 = (bf16[2,384,128]{2,1,0:T(8,128)(2,1)S(1)}, bf16[2,384,128]{2,1,0:T(8,128)(2,1)S(1)}, u32[]{:S(2)}, u32[]{:S(2)}) collective-permute-start(bf16[2,384,128]{2,1,0:T(8,128)(2,1)S(1)} %pad_maximum_fusion.refs_2_.refs_0_), channel_id=1, source_target_pairs={{0,384},{16,400},{32,416},{48,432},{64,448},{80,464},{96,480},{112... | collective-permute-start | bytes 589832 | tf_op jit(solution)/shard_map/ppermute | solution.py:30
  19.3 18.7 %collective-permute-start.3 = (bf16[2,384,128]{2,1,0:T(8,128)(2,1)S(1)}, bf16[2,384,128]{2,1,0:T(8,128)(2,1)S(1)}, u32[]{:S(2)}, u32[]{:S(2)}) collective-permute-start(bf16[2,384,128]{2,1,0:T(8,128)(2,1)S(1)} %pad_maximum_fusion.refs_2_.refs_0_), channel_id=1, source_target_pairs={{0,256},{16,272},{32,288},{48,304},{64,320},{80,336},{96,352},{112... | collective-permute-start | bytes 589832 | tf_op jit(solution)/shard_map/ppermute | solution.py:30
  21.6 18.7 %collective-permute-start.2 = (bf16[2,384,128]{2,1,0:T(8,128)(2,1)S(1)}, bf16[2,384,128]{2,1,0:T(8,128)(2,1)S(1)}, u32[]{:S(2)}, u32[]{:S(2)}) collective-permute-start(bf16[2,384,128]{2,1,0:T(8,128)(2,1)S(1)} %pad_maximum_fusion.refs_2_.refs_0_), channel_id=1, source_target_pairs={{0,128},{16,144},{32,160},{48,176},{64,192},{80,208},{96,224},{112... | collective-permute-start | bytes 589832 | tf_op jit(solution)/shard_map/ppermute | solution.py:30
  23.8 25.3 %collective-permute-start.9 = (bf16[128,2048]{1,0:T(8,128)(2,1)}, bf16[128,2048]{1,0:T(8,128)(2,1)S(1)}, u32[]{:S(2)}, u32[]{:S(2)}) collective-permute-start(bf16[128,2048]{1,0:T(8,128)(2,1)} %w0_ref.1), channel_id=1, source_target_pairs={{0,1},{1,0},{2,3},{3,2},{4,5},{5,4},{6,7},{7,6},{8,9},{9,8},{10,11... | collective-permute-start | bytes 1572872 | tf_op jit(solution)/shard_map/ppermute | solution.py:35
  27.7 0.9 copy-start.1
  28.7 14.0 %collective-permute-start.1 = (bf16[2,384,128]{2,1,0:T(8,128)(2,1)S(1)}, bf16[2,384,128]{2,1,0:T(8,128)(2,1)S(1)}, u32[]{:S(2)}, u32[]{:S(2)}) collective-permute-start(bf16[2,384,128]{2,1,0:T(8,128)(2,1)S(1)} %shard_map.46.refs_0_), channel_id=1, source_target_pairs={{0,16},{16,0},{32,48},{48,32},{64,80},{80,64},{96,112},{112,96},{1... | collective-permute-start | bytes 589832 | tf_op jit(solution)/shard_map/ppermute | solution.py:30
  33.2 13.2 %collective-permute-start.8 = (bf16[2,384,128]{2,1,0:T(8,128)(2,1)S(1)}, bf16[2,384,128]{2,1,0:T(8,128)(2,1)S(1)}, u32[]{:S(2)}, u32[]{:S(2)}) collective-permute-start(bf16[2,384,128]{2,1,0:T(8,128)(2,1)S(1)} %collective-permute-done.5.refs_2_.refs_4_), channel_id=1, source_target_pairs={{0,384},{16,400},{32,416},{48,432},{64,448},{80,464},{96,480},{112... | collective-permute-start | bytes 589832 | tf_op jit(solution)/shard_map/ppermute | solution.py:30
  38.0 8.4 %collective-permute-start.7 = (bf16[2,384,128]{2,1,0:T(8,128)(2,1)S(1)}, bf16[2,384,128]{2,1,0:T(8,128)(2,1)S(1)}, u32[]{:S(2)}, u32[]{:S(2)}) collective-permute-start(bf16[2,384,128]{2,1,0:T(8,128)(2,1)S(1)} %collective-permute-done.5.refs_2_.refs_4_), channel_id=1, source_target_pairs={{0,256},{16,272},{32,288},{48,304},{64,320},{80,336},{96,352},{112... | collective-permute-start | bytes 589832 | tf_op jit(solution)/shard_map/ppermute | solution.py:30
  40.3 8.8 %collective-permute-start.6 = (bf16[2,384,128]{2,1,0:T(8,128)(2,1)S(1)}, bf16[2,384,128]{2,1,0:T(8,128)(2,1)S(1)}, u32[]{:S(2)}, u32[]{:S(2)}) collective-permute-start(bf16[2,384,128]{2,1,0:T(8,128)(2,1)S(1)} %collective-permute-done.5.refs_2_.refs_4_), channel_id=1, source_target_pairs={{0,128},{16,144},{32,160},{48,176},{64,192},{80,208},{96,224},{112... | collective-permute-start | bytes 589832 | tf_op jit(solution)/shard_map/ppermute | solution.py:30
  82.1 23.1 %copy-start = (bf16[128,2048]{1,0:T(8,128)(2,1)S(1)}, bf16[128,2048]{1,0:T(8,128)(2,1)}, u32[]{:S(2)}) copy-start(bf16[128,2048]{1,0:T(8,128)(2,1)} %w0_ref.1) | copy-start | bytes 1572868
  96.6 8.5 %collective-permute-start.10 = (bf16[384,128]{1,0:T(8,128)(2,1)S(1)}, bf16[384,128]{1,0:T(8,128)(2,1)S(1)}, u32[]{:S(2)}, u32[]{:S(2)}) collective-permute-start(bf16[384,128]{1,0:T(8,128)(2,1)S(1)} %reduce_sum.21.own_ref), channel_id=1, source_target_pairs={{0,1},{1,0},{2,3},{3,2},{4,5},{5,4},{6,7},{7,6},{8,9},{9,8},{10,11... | collective-permute-start | bytes 294920 | tf_op jit(solution)/shard_map/ppermute | solution.py:35
  121.6 20.4 %collective-permute-start.11 = (bf16[384,128]{1,0:T(8,128)(2,1)S(1)}, bf16[384,128]{1,0:T(8,128)(2,1)S(1)}, u32[]{:S(2)}, u32[]{:S(2)}) collective-permute-start(bf16[384,128]{1,0:T(8,128)(2,1)S(1)} %slice.15), channel_id=1, source_target_pairs={{0,8},{1,9},{2,10},{3,11},{4,12},{5,13},{6,14},{7,15},{8,0},{9,1},... | collective-permute-start | bytes 294920 | tf_op jit(solution)/shard_map/ppermute | solution.py:35

commit v3 on v2

--- a/solution.py
+++ b/solution.py
@@ -242,7 +242,7 @@
     )(place, *expos, factor, *pieces, sums)
 
 
-def project_kernel(place_ref, own_ref, other_ref, w0_ref, w1_ref, out_ref, w_ref):
+def project_kernel(place_ref, own_ref, other_ref, w0_ref, w1_ref, near_ref, far_ref, w_ref):
     zh, core = place_ref[2], place_ref[4]
     for x in range(4):
         for dzh in range(2):
@@ -253,17 +253,17 @@
             w_ref[DIM:, at] = w1_ref[:, lanes]
     rows = jnp.concatenate([own_ref[...], other_ref[...]], axis=1)
     for x in range(4):
-        out_ref[x] = jnp.dot(
-            rows, w_ref[:, x * 256 : (x + 1) * 256], preferred_element_type=F32
-        ).astype(BF16)
+        part = jnp.dot(rows, w_ref[:, x * 256 : (x + 1) * 256], preferred_element_type=F32)
+        near_ref[x] = part[:, :128].astype(BF16)
+        far_ref[x] = part[:, 128:].astype(BF16)
 
 
 def project(place, own, other, w_own, w_other):
     return pl.pallas_call(
         project_kernel,
         in_specs=[SMEM] + [VMEM] * 4,
-        out_specs=VMEM,
-        out_shape=jax.ShapeDtypeStruct((4, ROWS, 256), BF16),
+        out_specs=[VMEM] * 2,
+        out_shape=[jax.ShapeDtypeStruct((4, ROWS, 128), BF16)] * 2,
         scratch_shapes=[pltpu.VMEM((2 * DIM, 1024), BF16)],
         compiler_params=pltpu.CompilerParams(vmem_limit_bytes=16 * 1024 * 1024),
     )(place, own, other, w_own, w_other)
@@ -306,10 +306,12 @@
     factor, sums = columns(place, expos, (stats_near, stats_far), swap(stats, "ctx", LINE))
     attended = attend(place, expos, factor, near_pieces + far_pieces, swap(sums, "ctx", PLANE))
     whole = jnp.sum(swap(attended, "ctx", LINE).astype(F32), axis=0).astype(BF16)
-    parts = project(place, whole, head_send(whole, dcore=1), out_weight, w_other)
-    both = jnp.sum(swap(parts, "head", ROW).astype(F32), axis=0)
-    far = head_send(both[:, 128:].astype(BF16), dzh=1)
-    return (both[:, :128] + far.astype(F32)).astype(BF16)
+    near, far = project(place, whole, head_send(whole, dcore=1), out_weight, w_other)
+    far = jnp.sum(swap(far, "head", ROW).astype(F32), axis=0).astype(BF16)
+    near, far = lax.optimization_barrier((near, far))
+    far = head_send(far, dzh=1)
+    near = jnp.sum(swap(near, "head", ROW).astype(F32), axis=0)
+    return (near + far.astype(F32)).astype(BF16)
 
 
 def solution(mesh):

time: 143 us -> 143 us (level)
  the two profiles are of different devices: /device:TPU:33 before, /device:TPU:35 now
where the time goes in v3:
time: 143 us
  starting transfers between devices  61.6 us (43%)
  blocking collectives  46.4 us (32%)
  Pallas kernels  16.8 us (12%)
  waiting for transfers between devices  15 us (10%)
  other arithmetic  1.8 us (1%)
    all_to_all x4, blocking collectives, swap(): lax.all_to_all(value, axis, 0, 0, axis_index_groups=groups, tiled=True)  46.4 us
    ppermute x9, starting transfers between devices, ctx_send(): return lax.ppermute(value, 'ctx', [(i, i ^ step) for i in range(32)])  36.5 us
    ppermute x3, starting transfers between devices, head_send(): return lax.ppermute(value, 'head', [(i, i ^ step) for i in range(16)])  20.4 us
    ppermute x3, waiting for transfers between devices, head_send(): return lax.ppermute(value, 'head', [(i, i ^ step) for i in range(16)])  12.3 us
    all_to_all x1, starting transfers between devices, swap(): lax.all_to_all(value, axis, 0, 0, axis_index_groups=groups, tiled=True)  4.62 us
    pallas_call x1, Pallas kernels, second_scores(): pl.pallas_call(second_score_kernel, in_specs=[SMEM] + [VMEM] * 7, out_spe...  4.41 us
    pallas_call x1, Pallas kernels, attend(): pl.pallas_call(value_kernel, grid=(QB,), in_specs=[SMEM, EXPO, EXPO] + [V...  4.4 us
    pallas_call x1, Pallas kernels, first_scores(): pl.pallas_call(first_score_kernel, in_specs=[VMEM] * 6, out_specs=[EXPO,...  3.79 us
  transfers between devices with their start and end apart: 13, of which 3 were waited for; matrix products, arithmetic and copies ran while one was open for 0% of the time, Pallas kernels for 3%

profile of v3, /device:TPU:35, one launch (start us, length us, event | category | flops | bytes accessed | tf_op | source)
XLA Modules:
  0.0 142.7 jit_solution(7356568142830884489)
XLA Ops:
  0.0 1.0 pad_maximum_fusion.refs_2_.refs_0_
  1.0 4.9 %collective-permute-start = (bf16[1,384,128]{2,1,0:T(8,128)(2,1)}, bf16[1,384,128]{2,1,0:T(8,128)(2,1)S(1)}, u32[]{:S(2)}, u32[]{:S(2)}) collective-permute-start(bf16[1,384,128]{2,1,0:T(8,128)(2,1)} %bitcast.8), channel_id=1, source_target_pairs={{0,32},{16,48},{32,0},{48,16},{64,96},{80,112},{96,64},{112,80},{1... | collective-permute-start | bytes 294920 | tf_op jit(solution)/shard_map/ppermute | solution.py:30
  5.9 8.8 %collective-permute-start.5 = (bf16[2,384,128]{2,1,0:T(8,128)(2,1)S(1)}, bf16[2,384,128]{2,1,0:T(8,128)(2,1)S(1)}, u32[]{:S(2)}, u32[]{:S(2)}) collective-permute-start(bf16[2,384,128]{2,1,0:T(8,128)(2,1)S(1)} %pad_maximum_fusion.refs_2_.refs_0_), channel_id=1, source_target_pairs={{0,64},{16,80},{32,96},{48,112},{64,0},{80,16},{96,32},{112,48},{1... | collective-permute-start | bytes 589832 | tf_op jit(solution)/shard_map/ppermute | solution.py:30
  14.7 4.6 %collective-permute-start.4 = (bf16[2,384,128]{2,1,0:T(8,128)(2,1)S(1)}, bf16[2,384,128]{2,1,0:T(8,128)(2,1)S(1)}, u32[]{:S(2)}, u32[]{:S(2)}) collective-permute-start(bf16[2,384,128]{2,1,0:T(8,128)(2,1)S(1)} %pad_maximum_fusion.refs_2_.refs_0_), channel_id=1, source_target_pairs={{0,384},{16,400},{32,416},{48,432},{64,448},{80,464},{96,480},{112... | collective-permute-start | bytes 589832 | tf_op jit(solution)/shard_map/ppermute | solution.py:30
  19.3 2.3 %collective-permute-start.3 = (bf16[2,384,128]{2,1,0:T(8,128)(2,1)S(1)}, bf16[2,384,128]{2,1,0:T(8,128)(2,1)S(1)}, u32[]{:S(2)}, u32[]{:S(2)}) collective-permute-start(bf16[2,384,128]{2,1,0:T(8,128)(2,1)S(1)} %pad_maximum_fusion.refs_2_.refs_0_), channel_id=1, source_target_pairs={{0,256},{16,272},{32,288},{48,304},{64,320},{80,336},{96,352},{112... | collective-permute-start | bytes 589832 | tf_op jit(solution)/shard_map/ppermute | solution.py:30
  21.6 2.1 %collective-permute-start.2 = (bf16[2,384,128]{2,1,0:T(8,128)(2,1)S(1)}, bf16[2,384,128]{2,1,0:T(8,128)(2,1)S(1)}, u32[]{:S(2)}, u32[]{:S(2)}) collective-permute-start(bf16[2,384,128]{2,1,0:T(8,128)(2,1)S(1)} %pad_maximum_fusion.refs_2_.refs_0_), channel_id=1, source_target_pairs={{0,128},{16,144},{32,160},{48,176},{64,192},{80,208},{96,224},{112... | collective-permute-start | bytes 589832 | tf_op jit(solution)/shard_map/ppermute | solution.py:30
  23.8 0.0 collective-permute-done.b_ref
  23.8 3.9 %collective-permute-start.9 = (bf16[128,2048]{1,0:T(8,128)(2,1)}, bf16[128,2048]{1,0:T(8,128)(2,1)S(1)}, u32[]{:S(2)}, u32[]{:S(2)}) collective-permute-start(bf16[128,2048]{1,0:T(8,128)(2,1)} %w0_ref.1), channel_id=1, source_target_pairs={{0,1},{1,0},{2,3},{3,2},{4,5},{5,4},{6,7},{7,6},{8,9},{9,8},{10,11... | collective-permute-start | bytes 1572872 | tf_op jit(solution)/shard_map/ppermute | solution.py:35
  27.7 0.0 copy-start.1
  27.7 0.9 copy-done.1
  28.6 0.0 collective-permute-done.5.refs_2_.refs_4_
  28.7 4.7 %collective-permute-start.1 = (bf16[2,384,128]{2,1,0:T(8,128)(2,1)S(1)}, bf16[2,384,128]{2,1,0:T(8,128)(2,1)S(1)}, u32[]{:S(2)}, u32[]{:S(2)}) collective-permute-start(bf16[2,384,128]{2,1,0:T(8,128)(2,1)S(1)} %shard_map.46.refs_0_), channel_id=1, source_target_pairs={{0,16},{16,0},{32,48},{48,32},{64,80},{80,64},{96,112},{112,96},{1... | collective-permute-start | bytes 589832 | tf_op jit(solution)/shard_map/ppermute | solution.py:30
  33.4 0.0 collective-permute-done.4.refs_5_.refs_3_
  33.4 4.6 %collective-permute-start.8 = (bf16[2,384,128]{2,1,0:T(8,128)(2,1)S(1)}, bf16[2,384,128]{2,1,0:T(8,128)(2,1)S(1)}, u32[]{:S(2)}, u32[]{:S(2)}) collective-permute-start(bf16[2,384,128]{2,1,0:T(8,128)(2,1)S(1)} %collective-permute-done.5.refs_2_.refs_4_), channel_id=1, source_target_pairs={{0,384},{16,400},{32,416},{48,432},{64,448},{80,464},{96,480},{112... | collective-permute-start | bytes 589832 | tf_op jit(solution)/shard_map/ppermute | solution.py:30
  38.0 0.0 collective-permute-done.3.refs_4_.refs_2_
  38.0 2.3 %collective-permute-start.7 = (bf16[2,384,128]{2,1,0:T(8,128)(2,1)S(1)}, bf16[2,384,128]{2,1,0:T(8,128)(2,1)S(1)}, u32[]{:S(2)}, u32[]{:S(2)}) collective-permute-start(bf16[2,384,128]{2,1,0:T(8,128)(2,1)S(1)} %collective-permute-done.5.refs_2_.refs_4_), channel_id=1, source_target_pairs={{0,256},{16,272},{32,288},{48,304},{64,320},{80,336},{96,352},{112... | collective-permute-start | bytes 589832 | tf_op jit(solution)/shard_map/ppermute | solution.py:30
  40.3 0.0 collective-permute-done.2.refs_3_.refs_1_
  40.3 2.1 %collective-permute-start.6 = (bf16[2,384,128]{2,1,0:T(8,128)(2,1)S(1)}, bf16[2,384,128]{2,1,0:T(8,128)(2,1)S(1)}, u32[]{:S(2)}, u32[]{:S(2)}) collective-permute-start(bf16[2,384,128]{2,1,0:T(8,128)(2,1)S(1)} %collective-permute-done.5.refs_2_.refs_4_), channel_id=1, source_target_pairs={{0,128},{16,144},{32,160},{48,176},{64,192},{80,208},{96,224},{112... | collective-permute-start | bytes 589832 | tf_op jit(solution)/shard_map/ppermute | solution.py:30
  42.5 0.1 stack.23.place_ref
  42.6 0.0 collective-permute-done.1.refs_1_
  42.6 3.8 %shard_map.47 = (bf16[1536,1536]{1,0:T(8,128)(2,1)S(1)}, f32[4,8,128]{2,1,0:T(8,128)S(1)}) custom-call(bf16[2,384,128]{2,1,0:T(8,128)(2,1)S(1)} %shard_map.46.refs_0_, bf16[2,384,128]{2,1,0:T(8,128)(2,1)S(1)} %collective-permute-done.1.refs_1_, bf16[2,384,128]{2,1,0:T(8,128)(2,1)S(1)} %pad_maximum_fusion.refs_2_.refs_0_, ...), custom_call_target="tpu_custom_call" | custom-call | tf_op jit(solution)/shard_map/pallas_call | solution.py:126
  46.4 0.0 collective-permute-done.8.refs_5_.refs_7_
  46.4 0.0 collective-permute-done.7.refs_4_.refs_6_
  46.4 2.7 %collective-permute-done.6.refs_3_.refs_5_ = bf16[2,384,128]{2,1,0:T(8,128)(2,1)S(1)} collective-permute-done((bf16[2,384,128]{2,1,0:T(8,128)(2,1)S(1)}, bf16[2,384,128]{2,1,0:T(8,128)(2,1)S(1)}, u32[]{:S(2)}, u32[]{:S(2)}) %collective-permute-start.6) | collective-permute-done | bytes 196640 | tf_op jit(solution)/shard_map/ppermute | solution.py:30
  49.1 0.0 collective-permute-done.9.w1_ref
  49.1 4.4 %shard_map.48 = (bf16[1536,1536]{1,0:T(8,128)(2,1)S(1)}, f32[4,8,128]{2,1,0:T(8,128)S(1)}, f32[4,4,8,128]{3,2,1,0:T(8,128)S(1)}) custom-call(s32[5]{0:T(128)S(1)} %stack.23.place_ref, bf16[2,384,128]{2,1,0:T(8,128)(2,1)S(1)} %shard_map.46.refs_0_, bf16[2,384,128]{2,1,0:T(8,128)(2,1)S(1)} %collective-permute-done.1.refs_1_, ...), custom_call_target="tpu_custom_call" | custom-call | tf_op jit(solution)/shard_map/pallas_call | solution.py:136
  53.5 6.4 %all_to_all.25.all_ref = f32[4,4,8,128]{3,2,1,0:T(8,128)S(1)} all-to-all(f32[4,4,8,128]{3,2,1,0:T(8,128)S(1)} %get-tuple-element.35), channel_id=1, replica_groups={{0,16,32,48},{64,80,96,112},{128,144,160,176},{192,208,224,240},{256,27..., dimensions={0} | all-to-all | bytes 131072 | tf_op jit(solution)/shard_map/all_to_all | solution.py:44
  59.9 2.3 %shard_map.49 = (f32[2,4,8,128]{3,2,1,0:T(8,128)S(1)}, f32[8,8,384]{2,1,0:T(8,128)S(1)}) custom-call(s32[5]{0:T(128)S(1)} %stack.23.place_ref, bf16[1536,1536]{1,0:T(8,128)(2,1)S(1)} %get-tuple-element.26.e0_ref, bf16[1536,1536]{1,0:T(8,128)(2,1)S(1)} %get-tuple-element.33.e1_ref, f32[4,8,128]{2,1,0:T(8,128)S(1)} %get-tuple-element.32.refs_6_.stat0_ref, ...), custom_call_target="tpu_custom_call" | custom-call | tf_op jit(solution)/shard_map/pallas_call | solution.py:184
  62.3 19.8 %all_to_all.26.refs_8_ = f32[8,8,384]{2,1,0:T(8,128)S(1)} all-to-all(f32[8,8,384]{2,1,0:T(8,128)S(1)} %get-tuple-element.37), channel_id=1, replica_groups={{0,64,128,192,256,320,384,448},{16,80,144,208,272,336,400,464},{32,96,1..., dimensions={0} | all-to-all | bytes 196608 | tf_op jit(solution)/shard_map/all_to_all | solution.py:44
  82.1 0.0 copy-start
  82.1 4.4 %shard_map.50 = bf16[4,384,128]{2,1,0:T(8,128)(2,1)S(1)} custom-call(s32[5]{0:T(128)S(1)} %stack.23.place_ref, bf16[1536,1536]{1,0:T(8,128)(2,1)S(1)} %get-tuple-element.26.e0_ref, bf16[1536,1536]{1,0:T(8,128)(2,1)S(1)} %get-tuple-element.33.e1_ref, f32[2,4,8,128]{3,2,1,0:T(8,128)S(1)} %get-tuple-element.36.factor_ref, ...), custom_call_target="tpu_custom_call" | custom-call | tf_op jit(solution)/shard_map/pallas_call | solution.py:234
  86.5 10.1 %all_to_all.27 = bf16[4,384,128]{2,1,0:T(8,128)(2,1)S(1)} all-to-all(bf16[4,384,128]{2,1,0:T(8,128)(2,1)S(1)} %shard_map.50), channel_id=1, replica_groups={{0,16,32,48},{64,80,96,112},{128,144,160,176},{192,208,224,240},{256,27..., dimensions={0} | all-to-all | bytes 786432 | tf_op jit(solution)/shard_map/all_to_all | solution.py:44
  96.6 0.1 reduce_sum.33.own_ref
  96.6 7.6 %collective-permute-start.10 = (bf16[384,128]{1,0:T(8,128)(2,1)S(1)}, bf16[384,128]{1,0:T(8,128)(2,1)S(1)}, u32[]{:S(2)}, u32[]{:S(2)}) collective-permute-start(bf16[384,128]{1,0:T(8,128)(2,1)S(1)} %reduce_sum.33.own_ref), channel_id=1, source_target_pairs={{0,1},{1,0},{2,3},{3,2},{4,5},{5,4},{6,7},{7,6},{8,9},{9,8},{10,11... | collective-permute-start | bytes 294920 | tf_op jit(solution)/shard_map/ppermute | solution.py:35
  104.2 0.9 collective-permute-done.10.other_ref
  105.1 0.0 copy-done
  105.1 1.8 %shard_map.51 = (bf16[4,384,128]{2,1,0:T(8,128)(2,1)}, bf16[4,384,128]{2,1,0:T(8,128)(2,1)S(1)}) custom-call(s32[5]{0:T(128)S(1)} %stack.23.place_ref, bf16[384,128]{1,0:T(8,128)(2,1)S(1)} %reduce_sum.33.own_ref, bf16[384,128]{1,0:T(8,128)(2,1)S(1)} %collective-permute-done.10.other_ref, bf16[128,2048]{1,0:T(8,128)(2,1)S(1)} %copy-done, ...), custom_call_target="tpu_custom_call" | custom-call | tf_op jit(solution)/shard_map/pallas_call | solution.py:262
  106.9 10.1 %all_to_all.28 = bf16[4,384,128]{2,1,0:T(8,128)(2,1)S(1)} all-to-all(bf16[4,384,128]{2,1,0:T(8,128)(2,1)S(1)} %get-tuple-element.40), channel_id=1, replica_groups={{0,2,4,6},{1,3,5,7},{8,10,12,14},{9,11,13,15},{16,18,20,22},{17,19,21,2..., dimensions={0} | all-to-all | bytes 786432 | tf_op jit(solution)/shard_map/all_to_all | solution.py:44
  117.0 0.1 reduce_sum.34
  117.1 4.6 %all-to-all-start.4 = ((bf16[4,384,128]{2,1,0:T(8,128)(2,1)}), bf16[4,384,128]{2,1,0:T(8,128)(2,1)S(1)}, u32[]{:S(2)}, u32[]{:S(2)}) async-start(bf16[4,384,128]{2,1,0:T(8,128)(2,1)} %get-tuple-element.41), calls=%async_computation.4 | async-start | bytes 786432 | tf_op jit(solution)/shard_map/all_to_all | solution.py:44
  121.7 8.9 %collective-permute-start.11 = (bf16[384,128]{1,0:T(8,128)(2,1)S(1)}, bf16[384,128]{1,0:T(8,128)(2,1)S(1)}, u32[]{:S(2)}, u32[]{:S(2)}) collective-permute-start(bf16[384,128]{1,0:T(8,128)(2,1)S(1)} %reduce_sum.34), channel_id=1, source_target_pairs={{0,8},{1,9},{2,10},{3,11},{4,12},{5,13},{6,14},{7,15},{8,0},{9,1},... | collective-permute-start | bytes 294920 | tf_op jit(solution)/shard_map/ppermute | solution.py:35
  130.7 0.0 all-to-all-done.4
  130.7 11.3 %collective-permute-done.11 = bf16[384,128]{1,0:T(8,128)(2,1)S(1)} collective-permute-done((bf16[384,128]{1,0:T(8,128)(2,1)S(1)}, bf16[384,128]{1,0:T(8,128)(2,1)S(1)}, u32[]{:S(2)}, u32[]{:S(2)}) %collective-permute-start.11) | collective-permute-done | bytes 98336 | tf_op jit(solution)/shard_map/ppermute | solution.py:35
  142.1 0.7 add_convert_fusion
  (2 shorter events, 0.1 us)
Async XLA Ops:
  1.0 22.8 %collective-permute-start = (bf16[1,384,128]{2,1,0:T(8,128)(2,1)}, bf16[1,384,128]{2,1,0:T(8,128)(2,1)S(1)}, u32[]{:S(2)}, u32[]{:S(2)}) collective-permute-start(bf16[1,384,128]{2,1,0:T(8,128)(2,1)} %bitcast.8), channel_id=1, source_target_pairs={{0,32},{16,48},{32,0},{48,16},{64,96},{80,112},{96,64},{112,80},{1... | collective-permute-start | bytes 294920 | tf_op jit(solution)/shard_map/ppermute | solution.py:30
  5.9 22.8 %collective-permute-start.5 = (bf16[2,384,128]{2,1,0:T(8,128)(2,1)S(1)}, bf16[2,384,128]{2,1,0:T(8,128)(2,1)S(1)}, u32[]{:S(2)}, u32[]{:S(2)}) collective-permute-start(bf16[2,384,128]{2,1,0:T(8,128)(2,1)S(1)} %pad_maximum_fusion.refs_2_.refs_0_), channel_id=1, source_target_pairs={{0,64},{16,80},{32,96},{48,112},{64,0},{80,16},{96,32},{112,48},{1... | collective-permute-start | bytes 589832 | tf_op jit(solution)/shard_map/ppermute | solution.py:30
  14.7 18.7 %collective-permute-start.4 = (bf16[2,384,128]{2,1,0:T(8,128)(2,1)S(1)}, bf16[2,384,128]{2,1,0:T(8,128)(2,1)S(1)}, u32[]{:S(2)}, u32[]{:S(2)}) collective-permute-start(bf16[2,384,128]{2,1,0:T(8,128)(2,1)S(1)} %pad_maximum_fusion.refs_2_.refs_0_), channel_id=1, source_target_pairs={{0,384},{16,400},{32,416},{48,432},{64,448},{80,464},{96,480},{112... | collective-permute-start | bytes 589832 | tf_op jit(solution)/shard_map/ppermute | solution.py:30
  19.3 18.7 %collective-permute-start.3 = (bf16[2,384,128]{2,1,0:T(8,128)(2,1)S(1)}, bf16[2,384,128]{2,1,0:T(8,128)(2,1)S(1)}, u32[]{:S(2)}, u32[]{:S(2)}) collective-permute-start(bf16[2,384,128]{2,1,0:T(8,128)(2,1)S(1)} %pad_maximum_fusion.refs_2_.refs_0_), channel_id=1, source_target_pairs={{0,256},{16,272},{32,288},{48,304},{64,320},{80,336},{96,352},{112... | collective-permute-start | bytes 589832 | tf_op jit(solution)/shard_map/ppermute | solution.py:30
  21.6 18.7 %collective-permute-start.2 = (bf16[2,384,128]{2,1,0:T(8,128)(2,1)S(1)}, bf16[2,384,128]{2,1,0:T(8,128)(2,1)S(1)}, u32[]{:S(2)}, u32[]{:S(2)}) collective-permute-start(bf16[2,384,128]{2,1,0:T(8,128)(2,1)S(1)} %pad_maximum_fusion.refs_2_.refs_0_), channel_id=1, source_target_pairs={{0,128},{16,144},{32,160},{48,176},{64,192},{80,208},{96,224},{112... | collective-permute-start | bytes 589832 | tf_op jit(solution)/shard_map/ppermute | solution.py:30
  23.8 25.3 %collective-permute-start.9 = (bf16[128,2048]{1,0:T(8,128)(2,1)}, bf16[128,2048]{1,0:T(8,128)(2,1)S(1)}, u32[]{:S(2)}, u32[]{:S(2)}) collective-permute-start(bf16[128,2048]{1,0:T(8,128)(2,1)} %w0_ref.1), channel_id=1, source_target_pairs={{0,1},{1,0},{2,3},{3,2},{4,5},{5,4},{6,7},{7,6},{8,9},{9,8},{10,11... | collective-permute-start | bytes 1572872 | tf_op jit(solution)/shard_map/ppermute | solution.py:35
  27.7 0.9 copy-start.1
  28.7 14.0 %collective-permute-start.1 = (bf16[2,384,128]{2,1,0:T(8,128)(2,1)S(1)}, bf16[2,384,128]{2,1,0:T(8,128)(2,1)S(1)}, u32[]{:S(2)}, u32[]{:S(2)}) collective-permute-start(bf16[2,384,128]{2,1,0:T(8,128)(2,1)S(1)} %shard_map.46.refs_0_), channel_id=1, source_target_pairs={{0,16},{16,0},{32,48},{48,32},{64,80},{80,64},{96,112},{112,96},{1... | collective-permute-start | bytes 589832 | tf_op jit(solution)/shard_map/ppermute | solution.py:30
  33.4 13.0 %collective-permute-start.8 = (bf16[2,384,128]{2,1,0:T(8,128)(2,1)S(1)}, bf16[2,384,128]{2,1,0:T(8,128)(2,1)S(1)}, u32[]{:S(2)}, u32[]{:S(2)}) collective-permute-start(bf16[2,384,128]{2,1,0:T(8,128)(2,1)S(1)} %collective-permute-done.5.refs_2_.refs_4_), channel_id=1, source_target_pairs={{0,384},{16,400},{32,416},{48,432},{64,448},{80,464},{96,480},{112... | collective-permute-start | bytes 589832 | tf_op jit(solution)/shard_map/ppermute | solution.py:30
  38.0 8.4 %collective-permute-start.7 = (bf16[2,384,128]{2,1,0:T(8,128)(2,1)S(1)}, bf16[2,384,128]{2,1,0:T(8,128)(2,1)S(1)}, u32[]{:S(2)}, u32[]{:S(2)}) collective-permute-start(bf16[2,384,128]{2,1,0:T(8,128)(2,1)S(1)} %collective-permute-done.5.refs_2_.refs_4_), channel_id=1, source_target_pairs={{0,256},{16,272},{32,288},{48,304},{64,320},{80,336},{96,352},{112... | collective-permute-start | bytes 589832 | tf_op jit(solution)/shard_map/ppermute | solution.py:30
  40.3 8.8 %collective-permute-start.6 = (bf16[2,384,128]{2,1,0:T(8,128)(2,1)S(1)}, bf16[2,384,128]{2,1,0:T(8,128)(2,1)S(1)}, u32[]{:S(2)}, u32[]{:S(2)}) collective-permute-start(bf16[2,384,128]{2,1,0:T(8,128)(2,1)S(1)} %collective-permute-done.5.refs_2_.refs_4_), channel_id=1, source_target_pairs={{0,128},{16,144},{32,160},{48,176},{64,192},{80,208},{96,224},{112... | collective-permute-start | bytes 589832 | tf_op jit(solution)/shard_map/ppermute | solution.py:30
  82.1 23.1 %copy-start = (bf16[128,2048]{1,0:T(8,128)(2,1)S(1)}, bf16[128,2048]{1,0:T(8,128)(2,1)}, u32[]{:S(2)}) copy-start(bf16[128,2048]{1,0:T(8,128)(2,1)} %w0_ref.1) | copy-start | bytes 1572868
  96.6 8.5 %collective-permute-start.10 = (bf16[384,128]{1,0:T(8,128)(2,1)S(1)}, bf16[384,128]{1,0:T(8,128)(2,1)S(1)}, u32[]{:S(2)}, u32[]{:S(2)}) collective-permute-start(bf16[384,128]{1,0:T(8,128)(2,1)S(1)} %reduce_sum.33.own_ref), channel_id=1, source_target_pairs={{0,1},{1,0},{2,3},{3,2},{4,5},{5,4},{6,7},{7,6},{8,9},{9,8},{10,11... | collective-permute-start | bytes 294920 | tf_op jit(solution)/shard_map/ppermute | solution.py:35
  117.1 13.6 %all-to-all-start.4 = ((bf16[4,384,128]{2,1,0:T(8,128)(2,1)}), bf16[4,384,128]{2,1,0:T(8,128)(2,1)S(1)}, u32[]{:S(2)}, u32[]{:S(2)}) async-start(bf16[4,384,128]{2,1,0:T(8,128)(2,1)} %get-tuple-element.41), calls=%async_computation.4 | async-start | bytes 786432 | tf_op jit(solution)/shard_map/all_to_all | solution.py:44
  121.7 20.3 %collective-permute-start.11 = (bf16[384,128]{1,0:T(8,128)(2,1)S(1)}, bf16[384,128]{1,0:T(8,128)(2,1)S(1)}, u32[]{:S(2)}, u32[]{:S(2)}) collective-permute-start(bf16[384,128]{1,0:T(8,128)(2,1)S(1)} %reduce_sum.34), channel_id=1, source_target_pairs={{0,8},{1,9},{2,10},{3,11},{4,12},{5,13},{6,14},{7,15},{8,0},{9,1},... | collective-permute-start | bytes 294920 | tf_op jit(solution)/shard_map/ppermute | solution.py:35

commit v4 on v3

--- a/solution.py
+++ b/solution.py
@@ -242,30 +242,29 @@
     )(place, *expos, factor, *pieces, sums)
 
 
-def project_kernel(place_ref, own_ref, other_ref, w0_ref, w1_ref, near_ref, far_ref, w_ref):
+def project_kernel(dzh, place_ref, own_ref, other_ref, w0_ref, w1_ref, out_ref, w_ref):
     zh, core = place_ref[2], place_ref[4]
     for x in range(4):
-        for dzh in range(2):
-            head = (zh ^ dzh) * 8 + x * 2 + core
-            lanes = pl.ds(pl.multiple_of(head * 128, 128), 128)
-            at = slice((x * 2 + dzh) * 128, (x * 2 + dzh + 1) * 128)
-            w_ref[:DIM, at] = w0_ref[:, lanes]
-            w_ref[DIM:, at] = w1_ref[:, lanes]
+        head = (zh ^ dzh) * 8 + x * 2 + core
+        lanes = pl.ds(pl.multiple_of(head * 128, 128), 128)
+        at = slice(x * 128, (x + 1) * 128)
+        w_ref[:DIM, at] = w0_ref[:, lanes]
+        w_ref[DIM:, at] = w1_ref[:, lanes]
     rows = jnp.concatenate([own_ref[...], other_ref[...]], axis=1)
+    part = jnp.dot(rows, w_ref[...], preferred_element_type=F32)
     for x in range(4):
-        part = jnp.dot(rows, w_ref[:, x * 256 : (x + 1) * 256], preferred_element_type=F32)
-        near_ref[x] = part[:, :128].astype(BF16)
-        far_ref[x] = part[:, 128:].astype(BF16)
-
-
-def project(place, own, other, w_own, w_other):
-    return pl.pallas_call(
-        project_kernel,
+        out_ref[x] = part[:, x * 128 : (x + 1) * 128].astype(BF16)
+
+
+def project(dzh, place, own, other, w_own, w_other):
+    return pl.pallas_call(
+        functools.partial(project_kernel, dzh),
         in_specs=[SMEM] + [VMEM] * 4,
-        out_specs=[VMEM] * 2,
-        out_shape=[jax.ShapeDtypeStruct((4, ROWS, 128), BF16)] * 2,
-        scratch_shapes=[pltpu.VMEM((2 * DIM, 1024), BF16)],
+        out_specs=VMEM,
+        out_shape=jax.ShapeDtypeStruct((4, ROWS, 128), BF16),
+        scratch_shapes=[pltpu.VMEM((2 * DIM, 512), BF16)],
         compiler_params=pltpu.CompilerParams(vmem_limit_bytes=16 * 1024 * 1024),
+        cost_estimate=pl.CostEstimate(flops=10**10, bytes_accessed=10**6, transcendentals=0),
     )(place, own, other, w_own, w_other)
 
 
@@ -306,10 +305,12 @@
     factor, sums = columns(place, expos, (stats_near, stats_far), swap(stats, "ctx", LINE))
     attended = attend(place, expos, factor, near_pieces + far_pieces, swap(sums, "ctx", PLANE))
     whole = jnp.sum(swap(attended, "ctx", LINE).astype(F32), axis=0).astype(BF16)
-    near, far = project(place, whole, head_send(whole, dcore=1), out_weight, w_other)
+    other = head_send(whole, dcore=1)
+    far = project(1, place, whole, other, out_weight, w_other)
     far = jnp.sum(swap(far, "head", ROW).astype(F32), axis=0).astype(BF16)
-    near, far = lax.optimization_barrier((near, far))
+    whole, other, far = lax.optimization_barrier((whole, other, far))
     far = head_send(far, dzh=1)
+    near = project(0, place, whole, other, out_weight, w_other)
     near = jnp.sum(swap(near, "head", ROW).astype(F32), axis=0)
     return (near + far.astype(F32)).astype(BF16)
 

time: 143 us -> 144 us (level)
  no operation moved by 1% of the time
where the time goes in v4:
time: 144 us; the launch traced here: 143 us
  starting transfers between devices  61.5 us (43%)
  blocking collectives  46.4 us (32%)
  Pallas kernels  17.5 us (12%)
  waiting for transfers between devices  15 us (10%)
  other arithmetic  1.8 us (1%)
    all_to_all x4, blocking collectives, swap(): lax.all_to_all(value, axis, 0, 0, axis_index_groups=groups, tiled=True)  46.4 us
    ppermute x9, starting transfers between devices, ctx_send(): return lax.ppermute(value, 'ctx', [(i, i ^ step) for i in range(32)])  36.5 us
    ppermute x3, starting transfers between devices, head_send(): return lax.ppermute(value, 'head', [(i, i ^ step) for i in range(16)])  20.4 us
    ppermute x3, waiting for transfers between devices, head_send(): return lax.ppermute(value, 'head', [(i, i ^ step) for i in range(16)])  12.3 us
    all_to_all x1, starting transfers between devices, swap(): lax.all_to_all(value, axis, 0, 0, axis_index_groups=groups, tiled=True)  4.61 us
    pallas_call x1, Pallas kernels, second_scores(): pl.pallas_call(second_score_kernel, in_specs=[SMEM] + [VMEM] * 7, out_spe...  4.41 us
    pallas_call x1, Pallas kernels, attend(): pl.pallas_call(value_kernel, grid=(QB,), in_specs=[SMEM, EXPO, EXPO] + [V...  4.4 us
    pallas_call x1, Pallas kernels, first_scores(): pl.pallas_call(first_score_kernel, in_specs=[VMEM] * 6, out_specs=[EXPO,...  3.79 us
  transfers between devices with their start and end apart: 13, of which 3 were waited for; matrix products, arithmetic and copies ran while one was open for 0% of the time, Pallas kernels for 3%

profile of v4, /device:TPU:35, one launch (start us, length us, event | category | flops | bytes accessed | tf_op | source)
XLA Modules:
  0.0 143.5 jit_solution(16990626362248000314)
XLA Ops:
  0.0 1.0 pad_maximum_fusion.refs_2_.refs_0_
  1.0 4.9 %collective-permute-start = (bf16[1,384,128]{2,1,0:T(8,128)(2,1)}, bf16[1,384,128]{2,1,0:T(8,128)(2,1)S(1)}, u32[]{:S(2)}, u32[]{:S(2)}) collective-permute-start(bf16[1,384,128]{2,1,0:T(8,128)(2,1)} %bitcast.8), channel_id=1, source_target_pairs={{0,32},{16,48},{32,0},{48,16},{64,96},{80,112},{96,64},{112,80},{1... | collective-permute-start | bytes 294920 | tf_op jit(solution)/shard_map/ppermute | solution.py:30
  5.9 8.8 %collective-permute-start.5 = (bf16[2,384,128]{2,1,0:T(8,128)(2,1)S(1)}, bf16[2,384,128]{2,1,0:T(8,128)(2,1)S(1)}, u32[]{:S(2)}, u32[]{:S(2)}) collective-permute-start(bf16[2,384,128]{2,1,0:T(8,128)(2,1)S(1)} %pad_maximum_fusion.refs_2_.refs_0_), channel_id=1, source_target_pairs={{0,64},{16,80},{32,96},{48,112},{64,0},{80,16},{96,32},{112,48},{1... | collective-permute-start | bytes 589832 | tf_op jit(solution)/shard_map/ppermute | solution.py:30
  14.7 4.6 %collective-permute-start.4 = (bf16[2,384,128]{2,1,0:T(8,128)(2,1)S(1)}, bf16[2,384,128]{2,1,0:T(8,128)(2,1)S(1)}, u32[]{:S(2)}, u32[]{:S(2)}) collective-permute-start(bf16[2,384,128]{2,1,0:T(8,128)(2,1)S(1)} %pad_maximum_fusion.refs_2_.refs_0_), channel_id=1, source_target_pairs={{0,384},{16,400},{32,416},{48,432},{64,448},{80,464},{96,480},{112... | collective-permute-start | bytes 589832 | tf_op jit(solution)/shard_map/ppermute | solution.py:30
  19.3 2.3 %collective-permute-start.3 = (bf16[2,384,128]{2,1,0:T(8,128)(2,1)S(1)}, bf16[2,384,128]{2,1,0:T(8,128)(2,1)S(1)}, u32[]{:S(2)}, u32[]{:S(2)}) collective-permute-start(bf16[2,384,128]{2,1,0:T(8,128)(2,1)S(1)} %pad_maximum_fusion.refs_2_.refs_0_), channel_id=1, source_target_pairs={{0,256},{16,272},{32,288},{48,304},{64,320},{80,336},{96,352},{112... | collective-permute-start | bytes 589832 | tf_op jit(solution)/shard_map/ppermute | solution.py:30
  21.6 2.1 %collective-permute-start.2 = (bf16[2,384,128]{2,1,0:T(8,128)(2,1)S(1)}, bf16[2,384,128]{2,1,0:T(8,128)(2,1)S(1)}, u32[]{:S(2)}, u32[]{:S(2)}) collective-permute-start(bf16[2,384,128]{2,1,0:T(8,128)(2,1)S(1)} %pad_maximum_fusion.refs_2_.refs_0_), channel_id=1, source_target_pairs={{0,128},{16,144},{32,160},{48,176},{64,192},{80,208},{96,224},{112... | collective-permute-start | bytes 589832 | tf_op jit(solution)/shard_map/ppermute | solution.py:30
  23.8 0.0 collective-permute-done.b_ref
  23.8 3.9 %collective-permute-start.9 = (bf16[128,2048]{1,0:T(8,128)(2,1)}, bf16[128,2048]{1,0:T(8,128)(2,1)S(1)}, u32[]{:S(2)}, u32[]{:S(2)}) collective-permute-start(bf16[128,2048]{1,0:T(8,128)(2,1)} %w0_ref.3), channel_id=1, source_target_pairs={{0,1},{1,0},{2,3},{3,2},{4,5},{5,4},{6,7},{7,6},{8,9},{9,8},{10,11... | collective-permute-start | bytes 1572872 | tf_op jit(solution)/shard_map/ppermute | solution.py:35
  27.7 0.0 copy-start.1
  27.7 0.9 copy-done.1
  28.6 0.0 collective-permute-done.5.refs_2_.refs_4_
  28.7 4.7 %collective-permute-start.1 = (bf16[2,384,128]{2,1,0:T(8,128)(2,1)S(1)}, bf16[2,384,128]{2,1,0:T(8,128)(2,1)S(1)}, u32[]{:S(2)}, u32[]{:S(2)}) collective-permute-start(bf16[2,384,128]{2,1,0:T(8,128)(2,1)S(1)} %shard_map.46.refs_0_), channel_id=1, source_target_pairs={{0,16},{16,0},{32,48},{48,32},{64,80},{80,64},{96,112},{112,96},{1... | collective-permute-start | bytes 589832 | tf_op jit(solution)/shard_map/ppermute | solution.py:30
  33.4 0.0 collective-permute-done.4.refs_5_.refs_3_
  33.4 4.6 %collective-permute-start.8 = (bf16[2,384,128]{2,1,0:T(8,128)(2,1)S(1)}, bf16[2,384,128]{2,1,0:T(8,128)(2,1)S(1)}, u32[]{:S(2)}, u32[]{:S(2)}) collective-permute-start(bf16[2,384,128]{2,1,0:T(8,128)(2,1)S(1)} %collective-permute-done.5.refs_2_.refs_4_), channel_id=1, source_target_pairs={{0,384},{16,400},{32,416},{48,432},{64,448},{80,464},{96,480},{112... | collective-permute-start | bytes 589832 | tf_op jit(solution)/shard_map/ppermute | solution.py:30
  38.0 0.0 collective-permute-done.3.refs_4_.refs_2_
  38.0 2.3 %collective-permute-start.7 = (bf16[2,384,128]{2,1,0:T(8,128)(2,1)S(1)}, bf16[2,384,128]{2,1,0:T(8,128)(2,1)S(1)}, u32[]{:S(2)}, u32[]{:S(2)}) collective-permute-start(bf16[2,384,128]{2,1,0:T(8,128)(2,1)S(1)} %collective-permute-done.5.refs_2_.refs_4_), channel_id=1, source_target_pairs={{0,256},{16,272},{32,288},{48,304},{64,320},{80,336},{96,352},{112... | collective-permute-start | bytes 589832 | tf_op jit(solution)/shard_map/ppermute | solution.py:30
  40.3 0.0 collective-permute-done.2.refs_3_.refs_1_
  40.3 2.1 %collective-permute-start.6 = (bf16[2,384,128]{2,1,0:T(8,128)(2,1)S(1)}, bf16[2,384,128]{2,1,0:T(8,128)(2,1)S(1)}, u32[]{:S(2)}, u32[]{:S(2)}) collective-permute-start(bf16[2,384,128]{2,1,0:T(8,128)(2,1)S(1)} %collective-permute-done.5.refs_2_.refs_4_), channel_id=1, source_target_pairs={{0,128},{16,144},{32,160},{48,176},{64,192},{80,208},{96,224},{112... | collective-permute-start | bytes 589832 | tf_op jit(solution)/shard_map/ppermute | solution.py:30
  42.5 0.1 stack.23.place_ref
  42.6 0.0 collective-permute-done.1.refs_1_
  42.6 3.8 %shard_map.47 = (bf16[1536,1536]{1,0:T(8,128)(2,1)S(1)}, f32[4,8,128]{2,1,0:T(8,128)S(1)}) custom-call(bf16[2,384,128]{2,1,0:T(8,128)(2,1)S(1)} %shard_map.46.refs_0_, bf16[2,384,128]{2,1,0:T(8,128)(2,1)S(1)} %collective-permute-done.1.refs_1_, bf16[2,384,128]{2,1,0:T(8,128)(2,1)S(1)} %pad_maximum_fusion.refs_2_.refs_0_, ...), custom_call_target="tpu_custom_call" | custom-call | tf_op jit(solution)/shard_map/pallas_call | solution.py:126
  46.4 0.0 collective-permute-done.8.refs_5_.refs_7_
  46.4 0.0 collective-permute-done.7.refs_4_.refs_6_
  46.4 2.7 %collective-permute-done.6.refs_3_.refs_5_ = bf16[2,384,128]{2,1,0:T(8,128)(2,1)S(1)} collective-permute-done((bf16[2,384,128]{2,1,0:T(8,128)(2,1)S(1)}, bf16[2,384,128]{2,1,0:T(8,128)(2,1)S(1)}, u32[]{:S(2)}, u32[]{:S(2)}) %collective-permute-start.6) | collective-permute-done | bytes 196640 | tf_op jit(solution)/shard_map/ppermute | solution.py:30
  49.1 0.0 collective-permute-done.9.w1_ref
  49.1 4.4 %shard_map.48 = (bf16[1536,1536]{1,0:T(8,128)(2,1)S(1)}, f32[4,8,128]{2,1,0:T(8,128)S(1)}, f32[4,4,8,128]{3,2,1,0:T(8,128)S(1)}) custom-call(s32[5]{0:T(128)S(1)} %stack.23.place_ref, bf16[2,384,128]{2,1,0:T(8,128)(2,1)S(1)} %shard_map.46.refs_0_, bf16[2,384,128]{2,1,0:T(8,128)(2,1)S(1)} %collective-permute-done.1.refs_1_, ...), custom_call_target="tpu_custom_call" | custom-call | tf_op jit(solution)/shard_map/pallas_call | solution.py:136
  53.5 6.4 %all_to_all.25.all_ref = f32[4,4,8,128]{3,2,1,0:T(8,128)S(1)} all-to-all(f32[4,4,8,128]{3,2,1,0:T(8,128)S(1)} %get-tuple-element.34), channel_id=1, replica_groups={{0,16,32,48},{64,80,96,112},{128,144,160,176},{192,208,224,240},{256,27..., dimensions={0} | all-to-all | bytes 131072 | tf_op jit(solution)/shard_map/all_to_all | solution.py:44
  59.9 2.3 %shard_map.49 = (f32[2,4,8,128]{3,2,1,0:T(8,128)S(1)}, f32[8,8,384]{2,1,0:T(8,128)S(1)}) custom-call(s32[5]{0:T(128)S(1)} %stack.23.place_ref, bf16[1536,1536]{1,0:T(8,128)(2,1)S(1)} %get-tuple-element.25.e0_ref, bf16[1536,1536]{1,0:T(8,128)(2,1)S(1)} %get-tuple-element.32.e1_ref, f32[4,8,128]{2,1,0:T(8,128)S(1)} %get-tuple-element.31.refs_6_.stat0_ref, ...), custom_call_target="tpu_custom_call" | custom-call | tf_op jit(solution)/shard_map/pallas_call | solution.py:184
  62.3 19.8 %all_to_all.26.refs_8_ = f32[8,8,384]{2,1,0:T(8,128)S(1)} all-to-all(f32[8,8,384]{2,1,0:T(8,128)S(1)} %get-tuple-element.36), channel_id=1, replica_groups={{0,64,128,192,256,320,384,448},{16,80,144,208,272,336,400,464},{32,96,1..., dimensions={0} | all-to-all | bytes 196608 | tf_op jit(solution)/shard_map/all_to_all | solution.py:44
  82.1 0.0 copy-start
  82.1 4.4 %shard_map.50 = bf16[4,384,128]{2,1,0:T(8,128)(2,1)S(1)} custom-call(s32[5]{0:T(128)S(1)} %stack.23.place_ref, bf16[1536,1536]{1,0:T(8,128)(2,1)S(1)} %get-tuple-element.25.e0_ref, bf16[1536,1536]{1,0:T(8,128)(2,1)S(1)} %get-tuple-element.32.e1_ref, f32[2,4,8,128]{3,2,1,0:T(8,128)S(1)} %get-tuple-element.35.factor_ref, ...), custom_call_target="tpu_custom_call" | custom-call | tf_op jit(solution)/shard_map/pallas_call | solution.py:234
  86.5 10.1 %all_to_all.27 = bf16[4,384,128]{2,1,0:T(8,128)(2,1)S(1)} all-to-all(bf16[4,384,128]{2,1,0:T(8,128)(2,1)S(1)} %shard_map.50), channel_id=1, replica_groups={{0,16,32,48},{64,80,96,112},{128,144,160,176},{192,208,224,240},{256,27..., dimensions={0} | all-to-all | bytes 786432 | tf_op jit(solution)/shard_map/all_to_all | solution.py:44
  96.6 0.1 reduce_sum.33.own_ref
  96.6 7.6 %collective-permute-start.10 = (bf16[384,128]{1,0:T(8,128)(2,1)S(1)}, bf16[384,128]{1,0:T(8,128)(2,1)S(1)}, u32[]{:S(2)}, u32[]{:S(2)}) collective-permute-start(bf16[384,128]{1,0:T(8,128)(2,1)S(1)} %reduce_sum.33.own_ref), channel_id=1, source_target_pairs={{0,1},{1,0},{2,3},{3,2},{4,5},{5,4},{6,7},{7,6},{8,9},{9,8},{10,11... | collective-permute-start | bytes 294920 | tf_op jit(solution)/shard_map/ppermute | solution.py:35
  104.2 0.9 collective-permute-done.10.other_ref
  105.1 0.0 copy-done
  105.1 0.9 shard_map.51
  106.0 10.1 %all_to_all.28 = bf16[4,384,128]{2,1,0:T(8,128)(2,1)S(1)} all-to-all(bf16[4,384,128]{2,1,0:T(8,128)(2,1)S(1)} %shard_map.51), channel_id=1, replica_groups={{0,2,4,6},{1,3,5,7},{8,10,12,14},{9,11,13,15},{16,18,20,22},{17,19,21,2..., dimensions={0} | all-to-all | bytes 786432 | tf_op jit(solution)/shard_map/all_to_all | solution.py:44
  116.1 0.1 reduce_sum.34
  116.2 1.6 %shard_map.52 = bf16[4,384,128]{2,1,0:T(8,128)(2,1)} custom-call(s32[5]{0:T(128)S(1)} %stack.23.place_ref, bf16[384,128]{1,0:T(8,128)(2,1)S(1)} %reduce_sum.33.own_ref, bf16[384,128]{1,0:T(8,128)(2,1)S(1)} %collective-permute-done.10.other_ref, bf16[128,2048]{1,0:T(8,128)(2,1)S(1)} %copy-done, bf16[128,2048]{1,0:T(8,128)(2,1)S(1)} %collective-permute-done.9.w1_ref), custom_call_target="tpu_custom_call" | custom-call | flops 10000000000 | bytes 1000000 | tf_op jit(solution)/shard_map/pallas_call | solution.py:260
  117.8 4.6 %all-to-all-start.4 = ((bf16[4,384,128]{2,1,0:T(8,128)(2,1)}), bf16[4,384,128]{2,1,0:T(8,128)(2,1)S(1)}, u32[]{:S(2)}, u32[]{:S(2)}) async-start(bf16[4,384,128]{2,1,0:T(8,128)(2,1)} %shard_map.52), calls=%async_computation.4 | async-start | bytes 786432 | tf_op jit(solution)/shard_map/all_to_all | solution.py:44
  122.5 8.9 %collective-permute-start.11 = (bf16[384,128]{1,0:T(8,128)(2,1)S(1)}, bf16[384,128]{1,0:T(8,128)(2,1)S(1)}, u32[]{:S(2)}, u32[]{:S(2)}) collective-permute-start(bf16[384,128]{1,0:T(8,128)(2,1)S(1)} %reduce_sum.34), channel_id=1, source_target_pairs={{0,8},{1,9},{2,10},{3,11},{4,12},{5,13},{6,14},{7,15},{8,0},{9,1},... | collective-permute-start | bytes 294920 | tf_op jit(solution)/shard_map/ppermute | solution.py:35
  131.4 0.0 all-to-all-done.4
  131.5 11.3 %collective-permute-done.11 = bf16[384,128]{1,0:T(8,128)(2,1)S(1)} collective-permute-done((bf16[384,128]{1,0:T(8,128)(2,1)S(1)}, bf16[384,128]{1,0:T(8,128)(2,1)S(1)}, u32[]{:S(2)}, u32[]{:S(2)}) %collective-permute-start.11) | collective-permute-done | bytes 98336 | tf_op jit(solution)/shard_map/ppermute | solution.py:35
  142.8 0.7 add_convert_fusion
  (2 shorter events, 0.1 us)
Async XLA Ops:
  1.0 22.8 %collective-permute-start = (bf16[1,384,128]{2,1,0:T(8,128)(2,1)}, bf16[1,384,128]{2,1,0:T(8,128)(2,1)S(1)}, u32[]{:S(2)}, u32[]{:S(2)}) collective-permute-start(bf16[1,384,128]{2,1,0:T(8,128)(2,1)} %bitcast.8), channel_id=1, source_target_pairs={{0,32},{16,48},{32,0},{48,16},{64,96},{80,112},{96,64},{112,80},{1... | collective-permute-start | bytes 294920 | tf_op jit(solution)/shard_map/ppermute | solution.py:30
  5.9 22.8 %collective-permute-start.5 = (bf16[2,384,128]{2,1,0:T(8,128)(2,1)S(1)}, bf16[2,384,128]{2,1,0:T(8,128)(2,1)S(1)}, u32[]{:S(2)}, u32[]{:S(2)}) collective-permute-start(bf16[2,384,128]{2,1,0:T(8,128)(2,1)S(1)} %pad_maximum_fusion.refs_2_.refs_0_), channel_id=1, source_target_pairs={{0,64},{16,80},{32,96},{48,112},{64,0},{80,16},{96,32},{112,48},{1... | collective-permute-start | bytes 589832 | tf_op jit(solution)/shard_map/ppermute | solution.py:30
  14.7 18.7 %collective-permute-start.4 = (bf16[2,384,128]{2,1,0:T(8,128)(2,1)S(1)}, bf16[2,384,128]{2,1,0:T(8,128)(2,1)S(1)}, u32[]{:S(2)}, u32[]{:S(2)}) collective-permute-start(bf16[2,384,128]{2,1,0:T(8,128)(2,1)S(1)} %pad_maximum_fusion.refs_2_.refs_0_), channel_id=1, source_target_pairs={{0,384},{16,400},{32,416},{48,432},{64,448},{80,464},{96,480},{112... | collective-permute-start | bytes 589832 | tf_op jit(solution)/shard_map/ppermute | solution.py:30
  19.3 18.7 %collective-permute-start.3 = (bf16[2,384,128]{2,1,0:T(8,128)(2,1)S(1)}, bf16[2,384,128]{2,1,0:T(8,128)(2,1)S(1)}, u32[]{:S(2)}, u32[]{:S(2)}) collective-permute-start(bf16[2,384,128]{2,1,0:T(8,128)(2,1)S(1)} %pad_maximum_fusion.refs_2_.refs_0_), channel_id=1, source_target_pairs={{0,256},{16,272},{32,288},{48,304},{64,320},{80,336},{96,352},{112... | collective-permute-start | bytes 589832 | tf_op jit(solution)/shard_map/ppermute | solution.py:30
  21.6 18.7 %collective-permute-start.2 = (bf16[2,384,128]{2,1,0:T(8,128)(2,1)S(1)}, bf16[2,384,128]{2,1,0:T(8,128)(2,1)S(1)}, u32[]{:S(2)}, u32[]{:S(2)}) collective-permute-start(bf16[2,384,128]{2,1,0:T(8,128)(2,1)S(1)} %pad_maximum_fusion.refs_2_.refs_0_), channel_id=1, source_target_pairs={{0,128},{16,144},{32,160},{48,176},{64,192},{80,208},{96,224},{112... | collective-permute-start | bytes 589832 | tf_op jit(solution)/shard_map/ppermute | solution.py:30
  23.8 25.3 %collective-permute-start.9 = (bf16[128,2048]{1,0:T(8,128)(2,1)}, bf16[128,2048]{1,0:T(8,128)(2,1)S(1)}, u32[]{:S(2)}, u32[]{:S(2)}) collective-permute-start(bf16[128,2048]{1,0:T(8,128)(2,1)} %w0_ref.3), channel_id=1, source_target_pairs={{0,1},{1,0},{2,3},{3,2},{4,5},{5,4},{6,7},{7,6},{8,9},{9,8},{10,11... | collective-permute-start | bytes 1572872 | tf_op jit(solution)/shard_map/ppermute | solution.py:35
  27.7 0.9 copy-start.1
  28.7 14.0 %collective-permute-start.1 = (bf16[2,384,128]{2,1,0:T(8,128)(2,1)S(1)}, bf16[2,384,128]{2,1,0:T(8,128)(2,1)S(1)}, u32[]{:S(2)}, u32[]{:S(2)}) collective-permute-start(bf16[2,384,128]{2,1,0:T(8,128)(2,1)S(1)} %shard_map.46.refs_0_), channel_id=1, source_target_pairs={{0,16},{16,0},{32,48},{48,32},{64,80},{80,64},{96,112},{112,96},{1... | collective-permute-start | bytes 589832 | tf_op jit(solution)/shard_map/ppermute | solution.py:30
  33.4 13.0 %collective-permute-start.8 = (bf16[2,384,128]{2,1,0:T(8,128)(2,1)S(1)}, bf16[2,384,128]{2,1,0:T(8,128)(2,1)S(1)}, u32[]{:S(2)}, u32[]{:S(2)}) collective-permute-start(bf16[2,384,128]{2,1,0:T(8,128)(2,1)S(1)} %collective-permute-done.5.refs_2_.refs_4_), channel_id=1, source_target_pairs={{0,384},{16,400},{32,416},{48,432},{64,448},{80,464},{96,480},{112... | collective-permute-start | bytes 589832 | tf_op jit(solution)/shard_map/ppermute | solution.py:30
  38.0 8.4 %collective-permute-start.7 = (bf16[2,384,128]{2,1,0:T(8,128)(2,1)S(1)}, bf16[2,384,128]{2,1,0:T(8,128)(2,1)S(1)}, u32[]{:S(2)}, u32[]{:S(2)}) collective-permute-start(bf16[2,384,128]{2,1,0:T(8,128)(2,1)S(1)} %collective-permute-done.5.refs_2_.refs_4_), channel_id=1, source_target_pairs={{0,256},{16,272},{32,288},{48,304},{64,320},{80,336},{96,352},{112... | collective-permute-start | bytes 589832 | tf_op jit(solution)/shard_map/ppermute | solution.py:30
  40.3 8.8 %collective-permute-start.6 = (bf16[2,384,128]{2,1,0:T(8,128)(2,1)S(1)}, bf16[2,384,128]{2,1,0:T(8,128)(2,1)S(1)}, u32[]{:S(2)}, u32[]{:S(2)}) collective-permute-start(bf16[2,384,128]{2,1,0:T(8,128)(2,1)S(1)} %collective-permute-done.5.refs_2_.refs_4_), channel_id=1, source_target_pairs={{0,128},{16,144},{32,160},{48,176},{64,192},{80,208},{96,224},{112... | collective-permute-start | bytes 589832 | tf_op jit(solution)/shard_map/ppermute | solution.py:30
  82.1 23.1 %copy-start = (bf16[128,2048]{1,0:T(8,128)(2,1)S(1)}, bf16[128,2048]{1,0:T(8,128)(2,1)}, u32[]{:S(2)}) copy-start(bf16[128,2048]{1,0:T(8,128)(2,1)} %w0_ref.3) | copy-start | bytes 1572868
  96.6 8.5 %collective-permute-start.10 = (bf16[384,128]{1,0:T(8,128)(2,1)S(1)}, bf16[384,128]{1,0:T(8,128)(2,1)S(1)}, u32[]{:S(2)}, u32[]{:S(2)}) collective-permute-start(bf16[384,128]{1,0:T(8,128)(2,1)S(1)} %reduce_sum.33.own_ref), channel_id=1, source_target_pairs={{0,1},{1,0},{2,3},{3,2},{4,5},{5,4},{6,7},{7,6},{8,9},{9,8},{10,11... | collective-permute-start | bytes 294920 | tf_op jit(solution)/shard_map/ppermute | solution.py:35
  117.8 13.6 %all-to-all-start.4 = ((bf16[4,384,128]{2,1,0:T(8,128)(2,1)}), bf16[4,384,128]{2,1,0:T(8,128)(2,1)S(1)}, u32[]{:S(2)}, u32[]{:S(2)}) async-start(bf16[4,384,128]{2,1,0:T(8,128)(2,1)} %shard_map.52), calls=%async_computation.4 | async-start | bytes 786432 | tf_op jit(solution)/shard_map/all_to_all | solution.py:44
  122.5 20.3 %collective-permute-start.11 = (bf16[384,128]{1,0:T(8,128)(2,1)S(1)}, bf16[384,128]{1,0:T(8,128)(2,1)S(1)}, u32[]{:S(2)}, u32[]{:S(2)}) collective-permute-start(bf16[384,128]{1,0:T(8,128)(2,1)S(1)} %reduce_sum.34), channel_id=1, source_target_pairs={{0,8},{1,9},{2,10},{3,11},{4,12},{5,13},{6,14},{7,15},{8,0},{9,1},... | collective-permute-start | bytes 294920 | tf_op jit(solution)/shard_map/ppermute | solution.py:35

commit v5 on v4

--- a/solution.py
+++ b/solution.py
@@ -309,10 +309,10 @@
     far = project(1, place, whole, other, out_weight, w_other)
     far = jnp.sum(swap(far, "head", ROW).astype(F32), axis=0).astype(BF16)
     whole, other, far = lax.optimization_barrier((whole, other, far))
-    far = head_send(far, dzh=1)
+    far = lax.optimization_barrier(head_send(far, dzh=1).astype(F32))
     near = project(0, place, whole, other, out_weight, w_other)
     near = jnp.sum(swap(near, "head", ROW).astype(F32), axis=0)
-    return (near + far.astype(F32)).astype(BF16)
+    return (near + far).astype(BF16)
 
 
 def solution(mesh):

time: 144 us -> 144 us (level)
  no operation moved by 1% of the time
where the time goes in v5:
time: 144 us
  starting transfers between devices  61.5 us (43%)
  blocking collectives  46.4 us (32%)
  Pallas kernels  17.5 us (12%)
  waiting for transfers between devices  15 us (10%)
  other arithmetic  1.8 us (1%)
    all_to_all x4, blocking collectives, swap(): lax.all_to_all(value, axis, 0, 0, axis_index_groups=groups, tiled=True)  46.4 us
    ppermute x9, starting transfers between devices, ctx_send(): return lax.ppermute(value, 'ctx', [(i, i ^ step) for i in range(32)])  36.5 us
    ppermute x3, starting transfers between devices, head_send(): return lax.ppermute(value, 'head', [(i, i ^ step) for i in range(16)])  20.4 us
    ppermute x3, waiting for transfers between devices, head_send(): return lax.ppermute(value, 'head', [(i, i ^ step) for i in range(16)])  12.3 us
    all_to_all x1, starting transfers between devices, swap(): lax.all_to_all(value, axis, 0, 0, axis_index_groups=groups, tiled=True)  4.61 us
    pallas_call x1, Pallas kernels, second_scores(): pl.pallas_call(second_score_kernel, in_specs=[SMEM] + [VMEM] * 7, out_spe...  4.41 us
    pallas_call x1, Pallas kernels, attend(): pl.pallas_call(value_kernel, grid=(QB,), in_specs=[SMEM, EXPO, EXPO] + [V...  4.4 us
    pallas_call x1, Pallas kernels, first_scores(): pl.pallas_call(first_score_kernel, in_specs=[VMEM] * 6, out_specs=[EXPO,...  3.79 us
  transfers between devices with their start and end apart: 13, of which 3 were waited for; matrix products, arithmetic and copies ran while one was open for 0% of the time, Pallas kernels for 3%

profile of v5, /device:TPU:35, one launch (start us, length us, event | category | flops | bytes accessed | tf_op | source)
XLA Modules:
  0.0 143.5 jit_solution(7747424508224378540)
XLA Ops:
  0.0 1.0 pad_maximum_fusion.refs_2_.refs_0_
  1.0 4.9 %collective-permute-start = (bf16[1,384,128]{2,1,0:T(8,128)(2,1)}, bf16[1,384,128]{2,1,0:T(8,128)(2,1)S(1)}, u32[]{:S(2)}, u32[]{:S(2)}) collective-permute-start(bf16[1,384,128]{2,1,0:T(8,128)(2,1)} %bitcast.8), channel_id=1, source_target_pairs={{0,32},{16,48},{32,0},{48,16},{64,96},{80,112},{96,64},{112,80},{1... | collective-permute-start | bytes 294920 | tf_op jit(solution)/shard_map/ppermute | solution.py:30
  5.9 8.8 %collective-permute-start.5 = (bf16[2,384,128]{2,1,0:T(8,128)(2,1)S(1)}, bf16[2,384,128]{2,1,0:T(8,128)(2,1)S(1)}, u32[]{:S(2)}, u32[]{:S(2)}) collective-permute-start(bf16[2,384,128]{2,1,0:T(8,128)(2,1)S(1)} %pad_maximum_fusion.refs_2_.refs_0_), channel_id=1, source_target_pairs={{0,64},{16,80},{32,96},{48,112},{64,0},{80,16},{96,32},{112,48},{1... | collective-permute-start | bytes 589832 | tf_op jit(solution)/shard_map/ppermute | solution.py:30
  14.7 4.6 %collective-permute-start.4 = (bf16[2,384,128]{2,1,0:T(8,128)(2,1)S(1)}, bf16[2,384,128]{2,1,0:T(8,128)(2,1)S(1)}, u32[]{:S(2)}, u32[]{:S(2)}) collective-permute-start(bf16[2,384,128]{2,1,0:T(8,128)(2,1)S(1)} %pad_maximum_fusion.refs_2_.refs_0_), channel_id=1, source_target_pairs={{0,384},{16,400},{32,416},{48,432},{64,448},{80,464},{96,480},{112... | collective-permute-start | bytes 589832 | tf_op jit(solution)/shard_map/ppermute | solution.py:30
  19.3 2.3 %collective-permute-start.3 = (bf16[2,384,128]{2,1,0:T(8,128)(2,1)S(1)}, bf16[2,384,128]{2,1,0:T(8,128)(2,1)S(1)}, u32[]{:S(2)}, u32[]{:S(2)}) collective-permute-start(bf16[2,384,128]{2,1,0:T(8,128)(2,1)S(1)} %pad_maximum_fusion.refs_2_.refs_0_), channel_id=1, source_target_pairs={{0,256},{16,272},{32,288},{48,304},{64,320},{80,336},{96,352},{112... | collective-permute-start | bytes 589832 | tf_op jit(solution)/shard_map/ppermute | solution.py:30
  21.6 2.1 %collective-permute-start.2 = (bf16[2,384,128]{2,1,0:T(8,128)(2,1)S(1)}, bf16[2,384,128]{2,1,0:T(8,128)(2,1)S(1)}, u32[]{:S(2)}, u32[]{:S(2)}) collective-permute-start(bf16[2,384,128]{2,1,0:T(8,128)(2,1)S(1)} %pad_maximum_fusion.refs_2_.refs_0_), channel_id=1, source_target_pairs={{0,128},{16,144},{32,160},{48,176},{64,192},{80,208},{96,224},{112... | collective-permute-start | bytes 589832 | tf_op jit(solution)/shard_map/ppermute | solution.py:30
  23.8 0.0 collective-permute-done.b_ref
  23.8 3.9 %collective-permute-start.9 = (bf16[128,2048]{1,0:T(8,128)(2,1)}, bf16[128,2048]{1,0:T(8,128)(2,1)S(1)}, u32[]{:S(2)}, u32[]{:S(2)}) collective-permute-start(bf16[128,2048]{1,0:T(8,128)(2,1)} %w0_ref.3), channel_id=1, source_target_pairs={{0,1},{1,0},{2,3},{3,2},{4,5},{5,4},{6,7},{7,6},{8,9},{9,8},{10,11... | collective-permute-start | bytes 1572872 | tf_op jit(solution)/shard_map/ppermute | solution.py:35
  27.7 0.0 copy-start.1
  27.7 0.9 copy-done.1
  28.6 0.0 collective-permute-done.5.refs_2_.refs_4_
  28.7 4.7 %collective-permute-start.1 = (bf16[2,384,128]{2,1,0:T(8,128)(2,1)S(1)}, bf16[2,384,128]{2,1,0:T(8,128)(2,1)S(1)}, u32[]{:S(2)}, u32[]{:S(2)}) collective-permute-start(bf16[2,384,128]{2,1,0:T(8,128)(2,1)S(1)} %shard_map.46.refs_0_), channel_id=1, source_target_pairs={{0,16},{16,0},{32,48},{48,32},{64,80},{80,64},{96,112},{112,96},{1... | collective-permute-start | bytes 589832 | tf_op jit(solution)/shard_map/ppermute | solution.py:30
  33.4 0.0 collective-permute-done.4.refs_5_.refs_3_
  33.4 4.6 %collective-permute-start.8 = (bf16[2,384,128]{2,1,0:T(8,128)(2,1)S(1)}, bf16[2,384,128]{2,1,0:T(8,128)(2,1)S(1)}, u32[]{:S(2)}, u32[]{:S(2)}) collective-permute-start(bf16[2,384,128]{2,1,0:T(8,128)(2,1)S(1)} %collective-permute-done.5.refs_2_.refs_4_), channel_id=1, source_target_pairs={{0,384},{16,400},{32,416},{48,432},{64,448},{80,464},{96,480},{112... | collective-permute-start | bytes 589832 | tf_op jit(solution)/shard_map/ppermute | solution.py:30
  38.0 0.0 collective-permute-done.3.refs_4_.refs_2_
  38.0 2.3 %collective-permute-start.7 = (bf16[2,384,128]{2,1,0:T(8,128)(2,1)S(1)}, bf16[2,384,128]{2,1,0:T(8,128)(2,1)S(1)}, u32[]{:S(2)}, u32[]{:S(2)}) collective-permute-start(bf16[2,384,128]{2,1,0:T(8,128)(2,1)S(1)} %collective-permute-done.5.refs_2_.refs_4_), channel_id=1, source_target_pairs={{0,256},{16,272},{32,288},{48,304},{64,320},{80,336},{96,352},{112... | collective-permute-start | bytes 589832 | tf_op jit(solution)/shard_map/ppermute | solution.py:30
  40.3 0.0 collective-permute-done.2.refs_3_.refs_1_
  40.3 2.1 %collective-permute-start.6 = (bf16[2,384,128]{2,1,0:T(8,128)(2,1)S(1)}, bf16[2,384,128]{2,1,0:T(8,128)(2,1)S(1)}, u32[]{:S(2)}, u32[]{:S(2)}) collective-permute-start(bf16[2,384,128]{2,1,0:T(8,128)(2,1)S(1)} %collective-permute-done.5.refs_2_.refs_4_), channel_id=1, source_target_pairs={{0,128},{16,144},{32,160},{48,176},{64,192},{80,208},{96,224},{112... | collective-permute-start | bytes 589832 | tf_op jit(solution)/shard_map/ppermute | solution.py:30
  42.5 0.1 stack.23.place_ref
  42.6 0.0 collective-permute-done.1.refs_1_
  42.6 3.8 %shard_map.47 = (bf16[1536,1536]{1,0:T(8,128)(2,1)S(1)}, f32[4,8,128]{2,1,0:T(8,128)S(1)}) custom-call(bf16[2,384,128]{2,1,0:T(8,128)(2,1)S(1)} %shard_map.46.refs_0_, bf16[2,384,128]{2,1,0:T(8,128)(2,1)S(1)} %collective-permute-done.1.refs_1_, bf16[2,384,128]{2,1,0:T(8,128)(2,1)S(1)} %pad_maximum_fusion.refs_2_.refs_0_, ...), custom_call_target="tpu_custom_call" | custom-call | tf_op jit(solution)/shard_map/pallas_call | solution.py:126
  46.4 0.0 collective-permute-done.8.refs_5_.refs_7_
  46.4 0.0 collective-permute-done.7.refs_4_.refs_6_
  46.4 2.7 %collective-permute-done.6.refs_3_.refs_5_ = bf16[2,384,128]{2,1,0:T(8,128)(2,1)S(1)} collective-permute-done((bf16[2,384,128]{2,1,0:T(8,128)(2,1)S(1)}, bf16[2,384,128]{2,1,0:T(8,128)(2,1)S(1)}, u32[]{:S(2)}, u32[]{:S(2)}) %collective-permute-start.6) | collective-permute-done | bytes 196640 | tf_op jit(solution)/shard_map/ppermute | solution.py:30
  49.1 0.0 collective-permute-done.9.w1_ref
  49.1 4.4 %shard_map.48 = (bf16[1536,1536]{1,0:T(8,128)(2,1)S(1)}, f32[4,8,128]{2,1,0:T(8,128)S(1)}, f32[4,4,8,128]{3,2,1,0:T(8,128)S(1)}) custom-call(s32[5]{0:T(128)S(1)} %stack.23.place_ref, bf16[2,384,128]{2,1,0:T(8,128)(2,1)S(1)} %shard_map.46.refs_0_, bf16[2,384,128]{2,1,0:T(8,128)(2,1)S(1)} %collective-permute-done.1.refs_1_, ...), custom_call_target="tpu_custom_call" | custom-call | tf_op jit(solution)/shard_map/pallas_call | solution.py:136
  53.5 6.4 %all_to_all.25.all_ref = f32[4,4,8,128]{3,2,1,0:T(8,128)S(1)} all-to-all(f32[4,4,8,128]{3,2,1,0:T(8,128)S(1)} %get-tuple-element.34), channel_id=1, replica_groups={{0,16,32,48},{64,80,96,112},{128,144,160,176},{192,208,224,240},{256,27..., dimensions={0} | all-to-all | bytes 131072 | tf_op jit(solution)/shard_map/all_to_all | solution.py:44
  59.9 2.3 %shard_map.49 = (f32[2,4,8,128]{3,2,1,0:T(8,128)S(1)}, f32[8,8,384]{2,1,0:T(8,128)S(1)}) custom-call(s32[5]{0:T(128)S(1)} %stack.23.place_ref, bf16[1536,1536]{1,0:T(8,128)(2,1)S(1)} %get-tuple-element.25.e0_ref, bf16[1536,1536]{1,0:T(8,128)(2,1)S(1)} %get-tuple-element.32.e1_ref, f32[4,8,128]{2,1,0:T(8,128)S(1)} %get-tuple-element.31.refs_6_.stat0_ref, ...), custom_call_target="tpu_custom_call" | custom-call | tf_op jit(solution)/shard_map/pallas_call | solution.py:184
  62.3 19.8 %all_to_all.26.refs_8_ = f32[8,8,384]{2,1,0:T(8,128)S(1)} all-to-all(f32[8,8,384]{2,1,0:T(8,128)S(1)} %get-tuple-element.36), channel_id=1, replica_groups={{0,64,128,192,256,320,384,448},{16,80,144,208,272,336,400,464},{32,96,1..., dimensions={0} | all-to-all | bytes 196608 | tf_op jit(solution)/shard_map/all_to_all | solution.py:44
  82.1 0.0 copy-start
  82.1 4.4 %shard_map.50 = bf16[4,384,128]{2,1,0:T(8,128)(2,1)S(1)} custom-call(s32[5]{0:T(128)S(1)} %stack.23.place_ref, bf16[1536,1536]{1,0:T(8,128)(2,1)S(1)} %get-tuple-element.25.e0_ref, bf16[1536,1536]{1,0:T(8,128)(2,1)S(1)} %get-tuple-element.32.e1_ref, f32[2,4,8,128]{3,2,1,0:T(8,128)S(1)} %get-tuple-element.35.factor_ref, ...), custom_call_target="tpu_custom_call" | custom-call | tf_op jit(solution)/shard_map/pallas_call | solution.py:234
  86.5 10.1 %all_to_all.27 = bf16[4,384,128]{2,1,0:T(8,128)(2,1)S(1)} all-to-all(bf16[4,384,128]{2,1,0:T(8,128)(2,1)S(1)} %shard_map.50), channel_id=1, replica_groups={{0,16,32,48},{64,80,96,112},{128,144,160,176},{192,208,224,240},{256,27..., dimensions={0} | all-to-all | bytes 786432 | tf_op jit(solution)/shard_map/all_to_all | solution.py:44
  96.6 0.1 reduce_sum.33.own_ref
  96.6 7.6 %collective-permute-start.10 = (bf16[384,128]{1,0:T(8,128)(2,1)S(1)}, bf16[384,128]{1,0:T(8,128)(2,1)S(1)}, u32[]{:S(2)}, u32[]{:S(2)}) collective-permute-start(bf16[384,128]{1,0:T(8,128)(2,1)S(1)} %reduce_sum.33.own_ref), channel_id=1, source_target_pairs={{0,1},{1,0},{2,3},{3,2},{4,5},{5,4},{6,7},{7,6},{8,9},{9,8},{10,11... | collective-permute-start | bytes 294920 | tf_op jit(solution)/shard_map/ppermute | solution.py:35
  104.2 0.9 collective-permute-done.10.other_ref
  105.1 0.0 copy-done
  105.1 0.9 shard_map.51
  106.0 10.1 %all_to_all.28 = bf16[4,384,128]{2,1,0:T(8,128)(2,1)S(1)} all-to-all(bf16[4,384,128]{2,1,0:T(8,128)(2,1)S(1)} %shard_map.51), channel_id=1, replica_groups={{0,2,4,6},{1,3,5,7},{8,10,12,14},{9,11,13,15},{16,18,20,22},{17,19,21,2..., dimensions={0} | all-to-all | bytes 786432 | tf_op jit(solution)/shard_map/all_to_all | solution.py:44
  116.1 0.1 reduce_sum.34
  116.2 1.6 %shard_map.52 = bf16[4,384,128]{2,1,0:T(8,128)(2,1)} custom-call(s32[5]{0:T(128)S(1)} %stack.23.place_ref, bf16[384,128]{1,0:T(8,128)(2,1)S(1)} %reduce_sum.33.own_ref, bf16[384,128]{1,0:T(8,128)(2,1)S(1)} %collective-permute-done.10.other_ref, bf16[128,2048]{1,0:T(8,128)(2,1)S(1)} %copy-done, bf16[128,2048]{1,0:T(8,128)(2,1)S(1)} %collective-permute-done.9.w1_ref), custom_call_target="tpu_custom_call" | custom-call | flops 10000000000 | bytes 1000000 | tf_op jit(solution)/shard_map/pallas_call | solution.py:260
  117.8 4.6 %all-to-all-start.4 = ((bf16[4,384,128]{2,1,0:T(8,128)(2,1)}), bf16[4,384,128]{2,1,0:T(8,128)(2,1)S(1)}, u32[]{:S(2)}, u32[]{:S(2)}) async-start(bf16[4,384,128]{2,1,0:T(8,128)(2,1)} %shard_map.52), calls=%async_computation.4 | async-start | bytes 786432 | tf_op jit(solution)/shard_map/all_to_all | solution.py:44
  122.5 8.9 %collective-permute-start.11 = (bf16[384,128]{1,0:T(8,128)(2,1)S(1)}, bf16[384,128]{1,0:T(8,128)(2,1)S(1)}, u32[]{:S(2)}, u32[]{:S(2)}) collective-permute-start(bf16[384,128]{1,0:T(8,128)(2,1)S(1)} %reduce_sum.34), channel_id=1, source_target_pairs={{0,8},{1,9},{2,10},{3,11},{4,12},{5,13},{6,14},{7,15},{8,0},{9,1},... | collective-permute-start | bytes 294920 | tf_op jit(solution)/shard_map/ppermute | solution.py:35
  131.4 11.4 %collective-permute-done.11 = bf16[384,128]{1,0:T(8,128)(2,1)S(1)} collective-permute-done((bf16[384,128]{1,0:T(8,128)(2,1)S(1)}, bf16[384,128]{1,0:T(8,128)(2,1)S(1)}, u32[]{:S(2)}, u32[]{:S(2)}) %collective-permute-start.11) | collective-permute-done | bytes 98336 | tf_op jit(solution)/shard_map/ppermute | solution.py:35
  142.8 0.0 all-to-all-done.4
  142.9 0.7 add_convert_fusion
  (3 shorter events, 0.1 us)
Async XLA Ops:
  1.0 22.8 %collective-permute-start = (bf16[1,384,128]{2,1,0:T(8,128)(2,1)}, bf16[1,384,128]{2,1,0:T(8,128)(2,1)S(1)}, u32[]{:S(2)}, u32[]{:S(2)}) collective-permute-start(bf16[1,384,128]{2,1,0:T(8,128)(2,1)} %bitcast.8), channel_id=1, source_target_pairs={{0,32},{16,48},{32,0},{48,16},{64,96},{80,112},{96,64},{112,80},{1... | collective-permute-start | bytes 294920 | tf_op jit(solution)/shard_map/ppermute | solution.py:30
  5.9 22.8 %collective-permute-start.5 = (bf16[2,384,128]{2,1,0:T(8,128)(2,1)S(1)}, bf16[2,384,128]{2,1,0:T(8,128)(2,1)S(1)}, u32[]{:S(2)}, u32[]{:S(2)}) collective-permute-start(bf16[2,384,128]{2,1,0:T(8,128)(2,1)S(1)} %pad_maximum_fusion.refs_2_.refs_0_), channel_id=1, source_target_pairs={{0,64},{16,80},{32,96},{48,112},{64,0},{80,16},{96,32},{112,48},{1... | collective-permute-start | bytes 589832 | tf_op jit(solution)/shard_map/ppermute | solution.py:30
  14.7 18.7 %collective-permute-start.4 = (bf16[2,384,128]{2,1,0:T(8,128)(2,1)S(1)}, bf16[2,384,128]{2,1,0:T(8,128)(2,1)S(1)}, u32[]{:S(2)}, u32[]{:S(2)}) collective-permute-start(bf16[2,384,128]{2,1,0:T(8,128)(2,1)S(1)} %pad_maximum_fusion.refs_2_.refs_0_), channel_id=1, source_target_pairs={{0,384},{16,400},{32,416},{48,432},{64,448},{80,464},{96,480},{112... | collective-permute-start | bytes 589832 | tf_op jit(solution)/shard_map/ppermute | solution.py:30
  19.3 18.7 %collective-permute-start.3 = (bf16[2,384,128]{2,1,0:T(8,128)(2,1)S(1)}, bf16[2,384,128]{2,1,0:T(8,128)(2,1)S(1)}, u32[]{:S(2)}, u32[]{:S(2)}) collective-permute-start(bf16[2,384,128]{2,1,0:T(8,128)(2,1)S(1)} %pad_maximum_fusion.refs_2_.refs_0_), channel_id=1, source_target_pairs={{0,256},{16,272},{32,288},{48,304},{64,320},{80,336},{96,352},{112... | collective-permute-start | bytes 589832 | tf_op jit(solution)/shard_map/ppermute | solution.py:30
  21.6 18.7 %collective-permute-start.2 = (bf16[2,384,128]{2,1,0:T(8,128)(2,1)S(1)}, bf16[2,384,128]{2,1,0:T(8,128)(2,1)S(1)}, u32[]{:S(2)}, u32[]{:S(2)}) collective-permute-start(bf16[2,384,128]{2,1,0:T(8,128)(2,1)S(1)} %pad_maximum_fusion.refs_2_.refs_0_), channel_id=1, source_target_pairs={{0,128},{16,144},{32,160},{48,176},{64,192},{80,208},{96,224},{112... | collective-permute-start | bytes 589832 | tf_op jit(solution)/shard_map/ppermute | solution.py:30
  23.8 25.3 %collective-permute-start.9 = (bf16[128,2048]{1,0:T(8,128)(2,1)}, bf16[128,2048]{1,0:T(8,128)(2,1)S(1)}, u32[]{:S(2)}, u32[]{:S(2)}) collective-permute-start(bf16[128,2048]{1,0:T(8,128)(2,1)} %w0_ref.3), channel_id=1, source_target_pairs={{0,1},{1,0},{2,3},{3,2},{4,5},{5,4},{6,7},{7,6},{8,9},{9,8},{10,11... | collective-permute-start | bytes 1572872 | tf_op jit(solution)/shard_map/ppermute | solution.py:35
  27.7 0.9 copy-start.1
  28.7 14.0 %collective-permute-start.1 = (bf16[2,384,128]{2,1,0:T(8,128)(2,1)S(1)}, bf16[2,384,128]{2,1,0:T(8,128)(2,1)S(1)}, u32[]{:S(2)}, u32[]{:S(2)}) collective-permute-start(bf16[2,384,128]{2,1,0:T(8,128)(2,1)S(1)} %shard_map.46.refs_0_), channel_id=1, source_target_pairs={{0,16},{16,0},{32,48},{48,32},{64,80},{80,64},{96,112},{112,96},{1... | collective-permute-start | bytes 589832 | tf_op jit(solution)/shard_map/ppermute | solution.py:30
  33.4 13.0 %collective-permute-start.8 = (bf16[2,384,128]{2,1,0:T(8,128)(2,1)S(1)}, bf16[2,384,128]{2,1,0:T(8,128)(2,1)S(1)}, u32[]{:S(2)}, u32[]{:S(2)}) collective-permute-start(bf16[2,384,128]{2,1,0:T(8,128)(2,1)S(1)} %collective-permute-done.5.refs_2_.refs_4_), channel_id=1, source_target_pairs={{0,384},{16,400},{32,416},{48,432},{64,448},{80,464},{96,480},{112... | collective-permute-start | bytes 589832 | tf_op jit(solution)/shard_map/ppermute | solution.py:30
  38.0 8.4 %collective-permute-start.7 = (bf16[2,384,128]{2,1,0:T(8,128)(2,1)S(1)}, bf16[2,384,128]{2,1,0:T(8,128)(2,1)S(1)}, u32[]{:S(2)}, u32[]{:S(2)}) collective-permute-start(bf16[2,384,128]{2,1,0:T(8,128)(2,1)S(1)} %collective-permute-done.5.refs_2_.refs_4_), channel_id=1, source_target_pairs={{0,256},{16,272},{32,288},{48,304},{64,320},{80,336},{96,352},{112... | collective-permute-start | bytes 589832 | tf_op jit(solution)/shard_map/ppermute | solution.py:30
  40.3 8.8 %collective-permute-start.6 = (bf16[2,384,128]{2,1,0:T(8,128)(2,1)S(1)}, bf16[2,384,128]{2,1,0:T(8,128)(2,1)S(1)}, u32[]{:S(2)}, u32[]{:S(2)}) collective-permute-start(bf16[2,384,128]{2,1,0:T(8,128)(2,1)S(1)} %collective-permute-done.5.refs_2_.refs_4_), channel_id=1, source_target_pairs={{0,128},{16,144},{32,160},{48,176},{64,192},{80,208},{96,224},{112... | collective-permute-start | bytes 589832 | tf_op jit(solution)/shard_map/ppermute | solution.py:30
  82.1 23.1 %copy-start = (bf16[128,2048]{1,0:T(8,128)(2,1)S(1)}, bf16[128,2048]{1,0:T(8,128)(2,1)}, u32[]{:S(2)}) copy-start(bf16[128,2048]{1,0:T(8,128)(2,1)} %w0_ref.3) | copy-start | bytes 1572868
  96.6 8.5 %collective-permute-start.10 = (bf16[384,128]{1,0:T(8,128)(2,1)S(1)}, bf16[384,128]{1,0:T(8,128)(2,1)S(1)}, u32[]{:S(2)}, u32[]{:S(2)}) collective-permute-start(bf16[384,128]{1,0:T(8,128)(2,1)S(1)} %reduce_sum.33.own_ref), channel_id=1, source_target_pairs={{0,1},{1,0},{2,3},{3,2},{4,5},{5,4},{6,7},{7,6},{8,9},{9,8},{10,11... | collective-permute-start | bytes 294920 | tf_op jit(solution)/shard_map/ppermute | solution.py:35
  117.8 25.0 %all-to-all-start.4 = ((bf16[4,384,128]{2,1,0:T(8,128)(2,1)}), bf16[4,384,128]{2,1,0:T(8,128)(2,1)S(1)}, u32[]{:S(2)}, u32[]{:S(2)}) async-start(bf16[4,384,128]{2,1,0:T(8,128)(2,1)} %shard_map.52), calls=%async_computation.4 | async-start | bytes 786432 | tf_op jit(solution)/shard_map/all_to_all | solution.py:44
  122.5 20.3 %collective-permute-start.11 = (bf16[384,128]{1,0:T(8,128)(2,1)S(1)}, bf16[384,128]{1,0:T(8,128)(2,1)S(1)}, u32[]{:S(2)}, u32[]{:S(2)}) collective-permute-start(bf16[384,128]{1,0:T(8,128)(2,1)S(1)} %reduce_sum.34), channel_id=1, source_target_pairs={{0,8},{1,9},{2,10},{3,11},{4,12},{5,13},{6,14},{7,15},{8,0},{9,1},... | collective-permute-start | bytes 294920 | tf_op jit(solution)/shard_map/ppermute | solution.py:35
